TPU v7x, 128 devices: a whole 4x4x4 slice. The times are simulated.
128 devices in a mesh: grp: 32 (over x, z, core), blk: 4 (over y).
Axes of the slice: x: 4, y: 4, z: 4, core: 2. Of those that a mesh axis runs over, the one named last changes fastest.
Arguments:
- embeddings: bfloat16 [131072, 1024], P(('grp', 'blk')), may hold values from -6 to 6
- labels: int32 [131072, 1], P(('grp', 'blk')), may hold values from 0 to 127; in each aligned block of 1024 rows (0 to 1023, 1024 to 2047, ...) at most 12 rows name the same one
- order_ids: int32 [131072], P(('grp', 'blk')), may hold values from 0 to 131071, each once
Outputs:
- best_match: float32 [131072], P(('grp', 'blk'))
Inputs may be any that keep to these rules, and one draw needn't show every extreme that they name: `labels`: among the 1024 documents of one device, no cluster holds more than 12; some cluster holds exactly 12 in some devices' rows. Every cluster has some document. `order_ids`: every place 0 to 131071 once.
All inputs are finite; a program needn't handle non-finite values.
Results may differ from a plain program's by a relative error of at most 0.0014.
Values may be sent and summed in bfloat16 or wider, within the bound.
No kernel may reach another device: no remote copies, remote signals or barrier semaphores. Data moves between devices by JAX's collectives and lax.ppermute only.
A program may use at most 64 MiB of HBM per device.

v0:
```python
import jax
import jax.numpy as jnp
from jax import lax
from jax.sharding import PartitionSpec as P

far_order = 1 << 30


def cluster_best(members, places):
    total_rows = members.shape[0]
    block_rows = min(512, total_rows)
    while total_rows % block_rows != 0:
        block_rows = block_rows // 2
    query_rows = members.reshape(total_rows // block_rows, block_rows, members.shape[1])
    query_places = places.reshape(total_rows // block_rows, block_rows)

    def one_block(pair):
        queries, query_order = pair
        scores = lax.dot_general(
            queries, members, (((1,), (1,)), ((), ())), preferred_element_type=jnp.float32
        )
        earlier = places[None, :] < query_order[:, None]
        return jnp.max(jnp.where(earlier, scores, jnp.float32(-1.0)), axis=1)

    return lax.map(one_block, (query_rows, query_places)).reshape(total_rows)


def shards(embeddings, labels, order_ids):
    rows = embeddings.shape[0]
    width = embeddings.shape[1]
    groups = lax.axis_size("grp")
    members_per = lax.axis_size("blk")
    devices = groups * members_per
    capacity = 3 * rows // (2 * devices)
    values = embeddings.astype(jnp.float32)
    scale = lax.rsqrt(jnp.mean(values * values, axis=1, keepdims=True) + 1e-06) * width ** (-0.5)
    unit = (values * scale).astype(jnp.bfloat16)
    label_flat = labels[:, 0]
    onehot = (label_flat[:, None] == jnp.arange(devices, dtype=jnp.int32)[None, :]).astype(
        jnp.int32
    )
    position = jnp.sum(jnp.cumsum(onehot, axis=0) * onehot, axis=1) - 1
    slots = label_flat * capacity + position
    outgoing = jnp.zeros((devices * capacity, width), jnp.bfloat16).at[slots].set(unit)
    out_order = jnp.full((devices * capacity,), far_order, jnp.int32).at[slots].set(order_ids)
    got_rows, got_order = (
        lax.all_to_all(
            outgoing.reshape(devices, capacity, width),
            ("grp", "blk"),
            split_axis=0,
            concat_axis=0,
            tiled=True,
        ),
        lax.all_to_all(
            out_order.reshape(devices, capacity),
            ("grp", "blk"),
            split_axis=0,
            concat_axis=0,
            tiled=True,
        ),
    )
    maxima = cluster_best(
        got_rows.reshape(devices * capacity, width), got_order.reshape(devices * capacity)
    )
    returned = lax.all_to_all(
        maxima.reshape(devices, capacity), ("grp", "blk"), split_axis=0, concat_axis=0, tiled=True
    )
    return returned.reshape(devices * capacity)[slots]


def solution(mesh):
    placed = (P(("grp", "blk"), None), P(("grp", "blk"), None), P(("grp", "blk")))
    return jax.shard_map(
        shards, mesh=mesh, in_specs=placed, out_specs=P(("grp", "blk")), check_vma=False
    )
```

profile of v0, /device:TPU:1, one launch (start us, length us, event | category | flops | bytes accessed | tf_op | source)
XLA Modules:
  0.0 140.6 jit_solution(3606879051764717633)
XLA Ops:
  0.0 0.9 copy.8
  1.3 1.0 fusion.10
  2.4 4.5 %scatter_custom_fusion = s32[1536]{0:T(1024)S(1)} fusion(s32[1024]{0:T(1024)S(1)} %bitcast.39, s32[1024]{0:T(1024)} %param.7, s32[]{:T(128)} %constant.42.clone.1), kind=kCustom, calls=%fused_computation.27 | custom fusion | bytes 6656 | tf_op jit(solution)/shard_map/scatter | solution.py:45
  6.9 0.7 all_to_all.17
  7.7 11.5 %all-to-all-start = ((s32[128,1,12]{2,1,0:T(1,128)}), s32[128,1,12]{2,1,0:T(1,128)S(1)}, u32[]{:S(2)}, u32[]{:S(2)}) async-start(s32[128,1,12]{2,1,0:T(1,128)} %bitcast.10), calls=%async_computation | async-start | bytes 131072 | tf_op jit(solution)/shard_map/all_to_all | solution.py:54
  19.2 0.5 fusion.4
  19.7 7.3 %scatter_custom_fusion.1 = bf16[1536,1024]{1,0:T(8,128)(2,1)S(1)} fusion(s32[1024]{0:T(1024)S(1)} %bitcast.40, bf16[1024,1024]{1,0:T(8,128)(2,1)} %param.5, f32[1024]{0:T(1024)S(1)} %rsqrt_multiply_fusion, bf16[]{:T(256)} %constant.9.clone.1), kind=kCustom, calls=%fused_computation.13 | custom fusion | flops 3145728 | bytes 5246978 | tf_op jit(solution)/shard_map/scatter | solution.py:44
  27.0 2.7 %reshape.57 = bf16[128,12,1024]{2,1,0:T(8,128)(2,1)} reshape(bf16[1536,1024]{1,0:T(8,128)(2,1)S(1)} %scatter_custom_fusion.1) | data formatting | bytes 6291456 | tf_op jit(solution)/shard_map/reshape | solution.py:48
  29.7 10.2 %all-to-all-start.1 = ((bf16[128,12,1024]{2,1,0:T(8,128)(2,1)}), bf16[128,12,1024]{2,1,0:T(8,128)(2,1)}, u32[]{:S(2)}, u32[]{:S(2)}) async-start(bf16[128,12,1024]{2,1,0:T(8,128)(2,1)} %reshape.57), calls=%async_computation.1 | async-start | bytes 8388608 | tf_op jit(solution)/shard_map/all_to_all | solution.py:47
  40.0 0.5 broadcast.71
  40.5 0.7 reduce.6
  41.3 51.7 %all-to-all-done.1 = bf16[128,12,1024]{2,1,0:T(8,128)(2,1)} async-done(((bf16[128,12,1024]{2,1,0:T(8,128)(2,1)}), bf16[128,12,1024]{2,1,0:T(8,128)(2,1)}, u32[]{:S(2)}, u32[]{:S(2)}) %all-to-all-start.1) | async-done | bytes 3145760 | tf_op jit(solution)/shard_map/all_to_all | solution.py:47
  93.0 4.7 %reshape.58 = bf16[1536,1024]{1,0:T(8,128)(2,1)S(1)} reshape(bf16[128,12,1024]{2,1,0:T(8,128)(2,1)} %all-to-all-done.1) | data formatting | bytes 6291456 | tf_op jit(solution)/shard_map/reshape | solution.py:63
  97.7 6.2 %reshape_reshape.8 = bf16[3,512,1024]{2,1,0:T(8,128)(2,1)} reshape(bf16[128,12,1024]{2,1,0:T(8,128)(2,1)} %all-to-all-done.1) | data formatting | bytes 6291456 | tf_op jit(solution)/shard_map/reshape;reshape | solution.py:14
  103.9 9.6 %while.11 = (s32[]{:T(128)}, f32[3,512]{1,0:T(4,128)S(1)}, s32[128,12]{1,0:T(8,128)}, s32[3,512]{1,0:T(4,128)S(1)}, bf16[3,512,1024]{2,1,0:T(8,128)(2,1)}, /*ind...) while((s32[]{:T(128)}, f32[3,512]{1,0:T(4,128)S(1)}, ...), condition=%wide.wide.region_8.9_spmd, body=%wide.wide.region_6.8_spmd.sunk | while | flops 1612971520 | bytes 4213349 | solution.py:25
  103.9 3.1 %fusion.25 = f32[512]{0:T(512)S(1)} fusion(bf16[1536,1024]{1,0:T(8,128)(2,1)S(1)} %get-tuple-element.140, s32[512]{0:T(512)S(1)} %bitcast.36, s32[1536]{0:T(1024)S(1)} %get-tuple-element.141, bf16[3,512,1024]{2,1,0:T(8,128)(2,1)} %get-tuple-element.139, s32[]{:T(128)} %get-tuple-element.126), kind=kOutput, calls=%fused_computation.4.clone.clone.1 | convolution fusion | flops 1612971520 | bytes 4205056 | tf_op jit(solution)/shard_map/while/body/eval_jaxpr/dot_general | solution.py:19
  107.1 3.1 %fusion.25 = f32[512]{0:T(512)S(1)} fusion(bf16[1536,1024]{1,0:T(8,128)(2,1)S(1)} %get-tuple-element.140, s32[512]{0:T(512)S(1)} %bitcast.36, s32[1536]{0:T(1024)S(1)} %get-tuple-element.141, bf16[3,512,1024]{2,1,0:T(8,128)(2,1)} %get-tuple-element.139, s32[]{:T(128)} %get-tuple-element.126), kind=kOutput, calls=%fused_computation.4.clone.clone.1 | convolution fusion | flops 1612971520 | bytes 4205056 | tf_op jit(solution)/shard_map/while/body/eval_jaxpr/dot_general | solution.py:19
  110.3 3.1 %fusion.25 = f32[512]{0:T(512)S(1)} fusion(bf16[1536,1024]{1,0:T(8,128)(2,1)S(1)} %get-tuple-element.140, s32[512]{0:T(512)S(1)} %bitcast.36, s32[1536]{0:T(1024)S(1)} %get-tuple-element.141, bf16[3,512,1024]{2,1,0:T(8,128)(2,1)} %get-tuple-element.139, s32[]{:T(128)} %get-tuple-element.126), kind=kOutput, calls=%fused_computation.4.clone.clone.1 | convolution fusion | flops 1612971520 | bytes 4205056 | tf_op jit(solution)/shard_map/while/body/eval_jaxpr/dot_general | solution.py:19
  113.5 0.7 all_to_all.21
  114.3 4.5 %all-to-all-start.2 = ((f32[128,1,12]{2,1,0:T(1,128)}), f32[128,1,12]{2,1,0:T(1,128)S(1)}, u32[]{:S(2)}, u32[]{:S(2)}) async-start(f32[128,1,12]{2,1,0:T(1,128)} %bitcast.12), calls=%async_computation.2 | async-start | bytes 131072 | tf_op jit(solution)/shard_map/all_to_all | solution.py:65
  118.8 9.9 %all-to-all-done.2 = f32[128,1,12]{2,1,0:T(1,128)S(1)} async-done(((f32[128,1,12]{2,1,0:T(1,128)}), f32[128,1,12]{2,1,0:T(1,128)S(1)}, u32[]{:S(2)}, u32[]{:S(2)}) %all-to-all-start.2) | async-done | bytes 6176 | tf_op jit(solution)/shard_map/all_to_all | solution.py:65
  128.7 0.5 broadcast.72
  129.2 0.8 reduce.7
  130.1 10.5 %gather_fusion = f32[1024]{0:T(1024)} fusion(f32[1536]{0:T(1024)S(1)} %reshape.59, s32[1024]{0:T(1024)S(1)} %broadcast_clamp_fusion), kind=kCustom, calls=%fused_computation | custom fusion | bytes 12288 | tf_op jit(solution)/shard_map/gather | solution.py:68
  (27 shorter events, 0.9 us)
Async XLA Ops:
  0.0 2.4 %copy-start.2 = (s32[1024,1]{0,1:T(1,128)S(1)}, s32[1024,1]{0,1:T(1,128)}, u32[]{:S(2)}) copy-start(s32[1024,1]{0,1:T(1,128)} %param.6) | copy-start | bytes 12292
  0.0 19.2 %copy-start = (bf16[1024,1024]{1,0:T(8,128)(2,1)S(1)}, bf16[1024,1024]{1,0:T(8,128)(2,1)}, u32[]{:S(2)}) copy-start(bf16[1024,1024]{1,0:T(8,128)(2,1)} %param.5) | copy-start | bytes 6291460
  7.7 22.0 %all-to-all-start = ((s32[128,1,12]{2,1,0:T(1,128)}), s32[128,1,12]{2,1,0:T(1,128)S(1)}, u32[]{:S(2)}, u32[]{:S(2)}) async-start(s32[128,1,12]{2,1,0:T(1,128)} %bitcast.10), calls=%async_computation | async-start | bytes 131072 | tf_op jit(solution)/shard_map/all_to_all | solution.py:54
  29.7 10.8 %copy-start.1 = (s32[128,1,12]{2,1,0:T(1,128)}, s32[128,1,12]{2,1,0:T(1,128)S(1)}, u32[]{:S(2)}) copy-start(s32[128,1,12]{2,1,0:T(1,128)S(1)} %all-to-all-done) | copy-start | bytes 18436
  29.7 63.3 %all-to-all-start.1 = ((bf16[128,12,1024]{2,1,0:T(8,128)(2,1)}), bf16[128,12,1024]{2,1,0:T(8,128)(2,1)}, u32[]{:S(2)}, u32[]{:S(2)}) async-start(bf16[128,12,1024]{2,1,0:T(8,128)(2,1)} %reshape.57), calls=%async_computation.1 | async-start | bytes 8388608 | tf_op jit(solution)/shard_map/all_to_all | solution.py:47
  114.3 14.4 %all-to-all-start.2 = ((f32[128,1,12]{2,1,0:T(1,128)}), f32[128,1,12]{2,1,0:T(1,128)S(1)}, u32[]{:S(2)}, u32[]{:S(2)}) async-start(f32[128,1,12]{2,1,0:T(1,128)} %bitcast.12), calls=%async_computation.2 | async-start | bytes 131072 | tf_op jit(solution)/shard_map/all_to_all | solution.py:65
where the time goes:
time: 141 us
  waiting for transfers between devices  61.6 us (44%)
  local copies, waits for them, and re-layouts  32.6 us (23%)
  starting transfers between devices  26.2 us (19%)
  other arithmetic  10.6 us (8%)
  matrix products  9.43 us (7%)
    all_to_all x1, waiting for transfers between devices, shards(): lax.all_to_all(outgoing.reshape(devices, capacity, width), ('grp', 'blk')...  51.7 us
    all_to_all x1, starting transfers between devices, shards(): lax.all_to_all(out_order.reshape(devices, capacity), ('grp', 'blk'), spli...  11.5 us
    gather x1, local copies, waits for them, and re-layouts, shards(): return returned.reshape(devices * capacity)[slots]  10.5 us
    all_to_all x1, starting transfers between devices, shards(): lax.all_to_all(outgoing.reshape(devices, capacity, width), ('grp', 'blk')...  10.2 us
    all_to_all x1, waiting for transfers between devices, shards(): lax.all_to_all(maxima.reshape(devices, capacity), ('grp', 'blk'), split_a...  9.88 us
    dot_general x3, matrix products, one_block(): lax.dot_general(queries, members, (((1,), (1,)), ((), ())), preferred_ele...  9.43 us
    scatter x1, other arithmetic, shards(): jnp.zeros((devices * capacity, width), jnp.bfloat16).at[slots].set(unit)  7.28 us
    another operation x1, local copies, waits for them, and re-layouts, cluster_best(): members.reshape(total_rows // block_rows, block_rows, members.shape[1])  6.17 us
  transfers between devices with their start and end apart: 3, of which 2 were waited for; matrix products, arithmetic and copies ran while one was open for 8% of the time, Pallas kernels for 0%

commit v1 on v0

v1 whole, which is shorter than its diff:
```python
import jax
import jax.numpy as jnp
from jax import lax
from jax.experimental import pallas as pl
from jax.experimental.pallas import tpu as pltpu
from jax.sharding import PartitionSpec as P

MAIN = 8
TAIL = 4
NT = (((1,), (1,)), ((), ()))
VMEM_LIMIT = 48 * 1024 * 1024


def fold_pair(low, high, upper):
    first = jnp.where(upper, pltpu.roll(high, 4, 0), low)
    second = jnp.where(upper, high, pltpu.roll(low, 4, 0))
    return first, second


def place_kernel(rows_ref, label_ref, order_ref, out_ref, position_ref, unit, digits, slots):
    step = pl.program_id(0)
    count, width = rows_ref.shape
    partners = out_ref.shape[0]
    devices = partners * pl.num_programs(0)

    @pl.when(step == 0)
    def _():
        labels = label_ref[...]
        carry = jnp.zeros((devices, 128), jnp.float32)
        inner = lax.broadcasted_iota(jnp.int32, (128, 256), 0)
        outer = lax.broadcasted_iota(jnp.int32, (128, 256), 1)
        before = ((inner < outer) | (outer >= 128)).astype(jnp.bfloat16)
        for block in range(count // 128):
            part = labels[:, block * 128 : (block + 1) * 128]
            member = lax.broadcasted_iota(jnp.int32, (devices, 128), 0) == part
            sums = jnp.dot(
                member.astype(jnp.bfloat16), before, preferred_element_type=jnp.float32
            )
            rank = jnp.where(member, sums[:, :128] + carry, 0.0)
            carry = carry + sums[:, 128:]
            position = jnp.sum(rank, axis=0, keepdims=True).astype(jnp.int32)
            position_ref[:, block * 128 : (block + 1) * 128] = position
            slots[0:1, block * 128 : (block + 1) * 128] = jnp.where(
                position < MAIN, part * MAIN + position, -1
            )
            slots[1:2, block * 128 : (block + 1) * 128] = jnp.where(
                position < MAIN, -1, part * TAIL + position - MAIN
            )
        order = order_ref[...]
        line = lax.broadcasted_iota(jnp.int32, (128, count), 0)
        digit = jnp.where(
            (line == 0) | (line == 4),
            order >> 12,
            jnp.where(
                (line == 1) | (line == 5),
                (order >> 6) & 63,
                jnp.where(
                    (line == 2) | (line == 6),
                    order & 63,
                    jnp.where((line == 3) | (line == 7), 1, 0),
                ),
            ),
        )
        digits[...] = digit.astype(jnp.float32).astype(jnp.bfloat16)
        for block in range(count // 128):
            values = rows_ref[block * 128 : (block + 1) * 128, :].astype(jnp.float32)
            scale = lax.rsqrt(
                jnp.mean(values * values, axis=1, keepdims=True) + 1e-06
            ) * width ** (-0.5)
            unit[block * 128 : (block + 1) * 128, :] = (values * scale).astype(jnp.bfloat16)

    slot = slots[...]
    main_rows, tail_rows = partners * MAIN, partners * TAIL
    main_at = lax.broadcasted_iota(jnp.int32, (main_rows, count), 0) + step * main_rows
    tail_at = lax.broadcasted_iota(jnp.int32, (tail_rows, count), 0) + step * tail_rows
    main_pick = (main_at == slot[0:1]).astype(jnp.bfloat16)
    tail_pick = (tail_at == slot[1:2]).astype(jnp.bfloat16)
    main = jnp.dot(main_pick, unit[...], preferred_element_type=jnp.float32)
    tail = jnp.dot(tail_pick, unit[...], preferred_element_type=jnp.float32)
    main_digits = lax.dot_general(
        main_pick, digits[...], NT, preferred_element_type=jnp.float32
    )
    tail_digits = lax.dot_general(
        tail_pick, digits[...], NT, preferred_element_type=jnp.float32
    )
    half = width // 2
    upper_half = lax.broadcasted_iota(jnp.int32, (8, half), 0) >= 4
    upper_line = lax.broadcasted_iota(jnp.int32, (8, 128), 0) >= 4
    left = lax.broadcasted_iota(jnp.int32, (8, 128), 1) < 4
    for partner in range(partners):
        out_ref[partner, :, :width] = main[partner * 8 : (partner + 1) * 8, :].astype(
            jnp.bfloat16
        )
    for pair in range(partners // 2):
        rows = tail[pair * 8 : (pair + 1) * 8, :]
        first, second = fold_pair(rows[:, :half], rows[:, half:], upper_half)
        out_ref[2 * pair, :, width : width + half] = first.astype(jnp.bfloat16)
        out_ref[2 * pair + 1, :, width : width + half] = second.astype(jnp.bfloat16)
        places = tail_digits[pair * 8 : (pair + 1) * 8, :]
        for odd, tail_part in ((0, places), (1, pltpu.roll(places, 4, 0))):
            partner = 2 * pair + odd
            both = jnp.where(
                left,
                main_digits[partner * 8 : (partner + 1) * 8, :],
                jnp.where(upper_line, 0.0, tail_part),
            )
            out_ref[partner, :, width + half :] = both.astype(jnp.bfloat16)


def score_kernel(got_ref, best_ref, member, digits, earlier_col, row_best, col_best):
    devices, _, total = got_ref.shape
    width = (total - 128) * 2 // 3
    half = width // 2
    main_rows, tail_rows = devices * MAIN, devices * TAIL
    docs = main_rows + tail_rows
    upper_half = lax.broadcasted_iota(jnp.int32, (8, half), 0) >= 4
    upper_line = lax.broadcasted_iota(jnp.int32, (8, 128), 0) >= 4
    lane = lax.broadcasted_iota(jnp.int32, (8, 128), 1)
    left = lane < 4
    for pair in range(devices // 2):
        a = got_ref[2 * pair, :, :].astype(jnp.float32)
        b = got_ref[2 * pair + 1, :, :].astype(jnp.float32)
        at = pair * 16
        member[at : at + 16, :] = jnp.concatenate([a[:, :width], b[:, :width]], axis=0).astype(
            jnp.bfloat16
        )
        a_digits, b_digits = a[:, width + half :], b[:, width + half :]
        digits[at : at + 16, :] = jnp.concatenate(
            [jnp.where(left, a_digits, 0.0), jnp.where(left, b_digits, 0.0)], axis=0
        ).astype(jnp.bfloat16)
    for quad in range(devices // 4):
        folded, places = [], []
        for pair in (2 * quad, 2 * quad + 1):
            a = got_ref[2 * pair, :, width:].astype(jnp.float32)
            b = got_ref[2 * pair + 1, :, width:].astype(jnp.float32)
            a_half, b_half = a[:, :half], b[:, :half]
            low = jnp.where(upper_half, pltpu.roll(b_half, 4, 0), a_half)
            high = jnp.where(upper_half, b_half, pltpu.roll(a_half, 4, 0))
            folded.append(jnp.concatenate([low, high], axis=1))
            both = jnp.where(upper_line, pltpu.roll(b[:, half:], 4, 0), a[:, half:])
            places.append(jnp.where(left, 0.0, both))
        at = main_rows + quad * 16
        member[at : at + 16, :] = jnp.concatenate(folded, axis=0).astype(jnp.bfloat16)
        digits[at : at + 16, :] = jnp.concatenate(places, axis=0).astype(jnp.bfloat16)

    def weights(shape, axis):
        line = lax.broadcasted_iota(jnp.int32, shape, axis)
        digit = line & 3
        weight = jnp.where(
            digit == 0,
            4096.0,
            jnp.where(digit == 1, 64.0, jnp.where(digit == 2, 1.0, -262144.0)),
        )
        return jnp.where(line < 8, weight, 0.0).astype(jnp.bfloat16)

    earlier_col[...] = jnp.dot(
        digits[...], weights((128, 128), 0), preferred_element_type=jnp.float32
    )
    place_row = lax.dot_general(
        weights((8, 128), 1), digits[...], NT, preferred_element_type=jnp.float32
    )
    step = 256
    row_best[...] = jnp.full_like(row_best, -1.0)
    col_best[...] = jnp.full_like(col_best, -1.0)
    for i in range(docs // step):
        mine = slice(i * step, (i + 1) * step)
        column = earlier_col[mine, :]
        for j in range(i + 1):
            theirs = slice(j * step, (j + 1) * step)
            scores = lax.dot_general(
                member[mine, :], member[theirs, :], NT, preferred_element_type=jnp.float32
            )
            best = row_best[mine, :]
            for k in range(step // 128):
                at = j * step + k * 128
                part = scores[:, k * 128 : (k + 1) * 128]
                row = place_row[0:1, at : at + 128]
                earlier = row < column
                best = jnp.maximum(best, jnp.where(earlier, part, -1.0))
                if j != i:
                    other = jnp.where(earlier, -1.0, part)
                    col_best[:, at : at + 128] = jnp.maximum(
                        col_best[:, at : at + 128],
                        jnp.max(other.reshape(step // 8, 8, 128), axis=0),
                    )
            row_best[mine, :] = best

    for block in range(docs // 128):
        at = block * 128
        column = jnp.max(col_best[:, at : at + 128], axis=0, keepdims=True)
        turned = jnp.broadcast_to(column, (128, 128)).T
        best = jnp.max(
            jnp.maximum(row_best[at : at + 128, :], turned), axis=1, keepdims=True
        )
        best = jnp.broadcast_to(best, (128, 128))
        line = lax.broadcasted_iota(jnp.int32, (128, 128), 0)
        lanes = lax.broadcasted_iota(jnp.int32, (128, 128), 1)
        if at < main_rows:
            kept = jnp.where(lanes == (line & 7), best, -2.0).reshape(16, 8, 128)
            best_ref[block * 16 : (block + 1) * 16, :] = jnp.max(kept, axis=1)
        else:
            kept = jnp.where(lanes == (line & 3) + MAIN, best, -2.0).reshape(32, 4, 128)
            first = (at - main_rows) // TAIL
            best_ref[first : first + 32, :] = jnp.maximum(
                best_ref[first : first + 32, :], jnp.max(kept, axis=1)
            )


def pick_kernel(got_ref, label_ref, position_ref, out_ref):
    devices = got_ref.shape[0]
    count = label_ref.shape[1]
    table = got_ref[...].T[:16, :]
    top = table.astype(jnp.bfloat16)
    rest = table - top.astype(jnp.float32)
    middle = rest.astype(jnp.bfloat16)
    low = (rest - middle.astype(jnp.float32)).astype(jnp.bfloat16)
    pick = (
        lax.broadcasted_iota(jnp.int32, (devices, count), 0) == label_ref[...]
    ).astype(jnp.bfloat16)

    def dot(part):
        return jnp.dot(part, pick, preferred_element_type=jnp.float32)

    values = (dot(top) + dot(middle)) + dot(low)
    line = lax.broadcasted_iota(jnp.int32, (16, count), 0)
    out_ref[...] = jnp.sum(
        jnp.where(line == position_ref[...], values, 0.0), axis=0, keepdims=True
    )


def shards(embeddings, labels, order_ids):
    rows, width = embeddings.shape
    devices = lax.axis_size("grp") * lax.axis_size("blk")
    total = width + width // 2 + 128
    docs = devices * (MAIN + TAIL)
    label_row = labels.reshape(1, rows)
    order_row = order_ids.reshape(1, rows)
    partners = 16
    params = pltpu.CompilerParams(vmem_limit_bytes=VMEM_LIMIT)

    def whole(*shape):
        return pl.BlockSpec(shape, lambda *_: (0,) * len(shape))

    outgoing, position = pl.pallas_call(
        place_kernel,
        grid=(devices // partners,),
        in_specs=[whole(rows, width), whole(1, rows), whole(1, rows)],
        out_specs=[
            pl.BlockSpec((partners, 8, total), lambda step: (step, 0, 0)),
            whole(1, rows),
        ],
        out_shape=[
            jax.ShapeDtypeStruct((devices, 8, total), jnp.bfloat16),
            jax.ShapeDtypeStruct((1, rows), jnp.int32),
        ],
        scratch_shapes=[
            pltpu.VMEM((rows, width), jnp.bfloat16),
            pltpu.VMEM((128, rows), jnp.bfloat16),
            pltpu.VMEM((8, rows), jnp.int32),
        ],
        compiler_params=params,
        name="place",
    )(embeddings, label_row, order_row)
    got = lax.all_to_all(outgoing, ("grp", "blk"), split_axis=0, concat_axis=0, tiled=True)
    best = pl.pallas_call(
        score_kernel,
        out_shape=jax.ShapeDtypeStruct((devices, 128), jnp.float32),
        scratch_shapes=[
            pltpu.VMEM((docs, width), jnp.bfloat16),
            pltpu.VMEM((docs, 128), jnp.bfloat16),
            pltpu.VMEM((docs, 128), jnp.float32),
            pltpu.VMEM((docs, 128), jnp.float32),
            pltpu.VMEM((8, docs), jnp.float32),
        ],
        compiler_params=params,
        name="score",
    )(got)
    returned = lax.all_to_all(
        best.reshape(devices, 1, 128), ("grp", "blk"), split_axis=0, concat_axis=0, tiled=True
    ).reshape(devices, 128)
    picked = pl.pallas_call(
        pick_kernel,
        out_shape=jax.ShapeDtypeStruct((1, rows), jnp.float32),
        compiler_params=params,
        name="pick",
    )(returned, label_row, position)
    return picked.reshape(rows)


def solution(mesh):
    placed = (P(("grp", "blk"), None), P(("grp", "blk"), None), P(("grp", "blk")))
    return jax.shard_map(
        shards, mesh=mesh, in_specs=placed, out_specs=P(("grp", "blk")), check_vma=False
    )
```

time: 141 us -> 86.5 us (0.61)
  blocking collectives: 0 us -> 70 us
  waiting for transfers between devices: 61.6 us -> 0 us
  local copies, waits for them, and re-layouts: 32.6 us -> 2.97 us
  starting transfers between devices: 26.2 us -> 0 us
  Pallas kernels: 0 us -> 13.3 us
  other arithmetic: 10.6 us -> 0 us
  matrix products: 9.43 us -> 0 us
    all_to_all x0 -> x2, blocking collectives: none -> 70 us  [the longest x1 56.3 us: shards(): lax.all_to_all(outgoing, ('grp', 'blk'), split_axis=0, concat_axis=0, til...]
    all_to_all x3 -> x0, waiting for transfers between devices: 61.6 us -> none  [the longest x1 51.7 us: shards(): lax.all_to_all(outgoing.reshape(devices, capacity, width), ('grp', 'blk')...]
    all_to_all x3 -> x0, starting transfers between devices: 26.2 us -> none  [the longest x1 11.5 us: shards(): lax.all_to_all(out_order.reshape(devices, capacity), ('grp', 'blk'), spli...]
    pallas_call x0 -> x3, Pallas kernels: none -> 13.3 us  [the longest x1 8.62 us: shards(): pl.pallas_call(place_kernel, grid=(devices // partners,), in_specs=[whole...]
    gather x1 -> x0, local copies, waits for them, and re-layouts: 10.5 us -> none  [shards(): return returned.reshape(devices * capacity)[slots]]
    dot_general x3 -> x0, matrix products: 9.43 us -> none  [one_block(): lax.dot_general(queries, members, (((1,), (1,)), ((), ())), preferred_ele...]
    reshape x3 -> x0, local copies, waits for them, and re-layouts: 7.51 us -> none  [the longest x1 4.71 us: shards(): got_rows.reshape(devices * capacity, width)]
    scatter x1 -> x0, other arithmetic: 7.28 us -> none  [shards(): jnp.zeros((devices * capacity, width), jnp.bfloat16).at[slots].set(unit)]
  transfers between devices with their start and end apart: 3 -> 0, of which waited for: 2 -> 0; matrix products, arithmetic and copies ran while one was open for 8% -> 0% of each run, Pallas kernels for 0% -> 0%
where the time goes in v1:
time: 86.5 us; the launch traced here: 86.3 us
  blocking collectives  70 us (81%)
  Pallas kernels  13.3 us (15%)
  local copies, waits for them, and re-layouts  2.97 us (3%)
    all_to_all x1, blocking collectives, shards(): lax.all_to_all(outgoing, ('grp', 'blk'), split_axis=0, concat_axis=0, til...  56.3 us
    all_to_all x1, blocking collectives, shards(): lax.all_to_all(best.reshape(devices, 1, 128), ('grp', 'blk'), split_axis=...  13.6 us
    pallas_call x1, Pallas kernels, shards(): pl.pallas_call(place_kernel, grid=(devices // partners,), in_specs=[whole...  8.62 us
    pallas_call x1, Pallas kernels, shards(): pl.pallas_call(score_kernel, out_shape=jax.ShapeDtypeStruct((devices, 128...  3.82 us
    unnamed x8, local copies, waits for them, and re-layouts  2.97 us

profile of v1, /device:TPU:1, one launch (start us, length us, event | category | flops | bytes accessed | tf_op | source)
XLA Modules:
  0.0 86.3 jit_solution(9126840968513817058)
XLA Ops:
  0.0 0.0 copy-start
  0.0 1.6 %copy-done = bf16[1024,1024]{1,0:T(8,128)(2,1)S(1)} copy-done((bf16[1024,1024]{1,0:T(8,128)(2,1)S(1)}, bf16[1024,1024]{1,0:T(8,128)(2,1)}, u32[]{:S(2)}) %copy-start) | copy-done | bytes 2097176
  1.6 0.0 copy-start.1
  1.6 0.7 copy-done.1
  2.3 0.0 copy-start.3
  2.3 0.7 copy-done.3
  3.0 8.6 %place.1 = (bf16[128,8,1664]{2,1,0:T(8,128)(2,1)S(1)}, s32[1,1024]{1,0:T(1,128)S(1)}) custom-call(bf16[1024,1024]{1,0:T(8,128)(2,1)S(1)} %copy-done, s32[1,1024]{1,0:T(1,128)S(1)} %bitcast.9, s32[1,1024]{1,0:T(1,128)S(1)} %bitcast.11), custom_call_target="tpu_custom_call" | custom-call | tf_op jit(solution)/shard_map/place/pallas_call | solution.py:244
  11.6 56.3 %all_to_all.10.got_ref = bf16[128,8,1664]{2,1,0:T(8,128)(2,1)S(1)} all-to-all(bf16[128,8,1664]{2,1,0:T(8,128)(2,1)S(1)} %get-tuple-element.7), channel_id=1, replica_groups=mesh['grp'=32,'blk'=4] {'grp','blk'}, dimensions={0} | all-to-all | bytes 6815744 | tf_op jit(solution)/shard_map/all_to_all | solution.py:264
  67.9 0.0 copy-start.2
  67.9 3.8 %score.1 = f32[128,128]{1,0:T(8,128)S(1)} custom-call(bf16[128,8,1664]{2,1,0:T(8,128)(2,1)S(1)} %all_to_all.10.got_ref), custom_call_target="tpu_custom_call" | custom-call | tf_op jit(solution)/shard_map/score/pallas_call | solution.py:265
  71.8 13.6 %all_to_all.11 = f32[128,1,128]{2,1,0:T(1,128)S(1)} all-to-all(f32[128,1,128]{2,1,0:T(1,128)S(1)} %bitcast.7), channel_id=1, replica_groups=mesh['grp'=32,'blk'=4] {'grp','blk'}, dimensions={0} | all-to-all | bytes 131072 | tf_op jit(solution)/shard_map/all_to_all | solution.py:278
  85.4 0.0 copy-done.2
  85.4 0.9 %pick.1 = f32[1,1024]{1,0:T(1,128)} custom-call(f32[128,128]{1,0:T(8,128)S(1)} %bitcast.8, s32[1,1024]{1,0:T(1,128)S(1)} %bitcast.10, s32[1,1024]{1,0:T(1,128)S(1)} %get-tuple-element.8.position_ref), custom_call_target="tpu_custom_call" | custom-call | tf_op jit(solution)/shard_map/pick/pallas_call | solution.py:281
Async XLA Ops:
  0.0 1.6 %copy-start = (bf16[1024,1024]{1,0:T(8,128)(2,1)S(1)}, bf16[1024,1024]{1,0:T(8,128)(2,1)}, u32[]{:S(2)}) copy-start(bf16[1024,1024]{1,0:T(8,128)(2,1)} %rows_ref.1) | copy-start | bytes 6291460
  1.6 0.7 copy-start.1
  2.3 0.7 copy-start.3
  67.9 17.5 %copy-start.2 = (s32[1024,1]{0,1:T(1,128)S(1)}, s32[1024,1]{0,1:T(1,128)}, u32[]{:S(2)}) copy-start(s32[1024,1]{0,1:T(1,128)} %param.4) | copy-start | bytes 12292

commit v2 on v1

--- a/solution.py
+++ b/solution.py
@@ -11,100 +11,121 @@
 VMEM_LIMIT = 48 * 1024 * 1024
 
 
-def fold_pair(low, high, upper):
-    first = jnp.where(upper, pltpu.roll(high, 4, 0), low)
-    second = jnp.where(upper, high, pltpu.roll(low, 4, 0))
-    return first, second
-
-
-def place_kernel(rows_ref, label_ref, order_ref, out_ref, position_ref, unit, digits, slots):
-    step = pl.program_id(0)
-    count, width = rows_ref.shape
-    partners = out_ref.shape[0]
-    devices = partners * pl.num_programs(0)
-
-    @pl.when(step == 0)
-    def _():
-        labels = label_ref[...]
-        carry = jnp.zeros((devices, 128), jnp.float32)
-        inner = lax.broadcasted_iota(jnp.int32, (128, 256), 0)
-        outer = lax.broadcasted_iota(jnp.int32, (128, 256), 1)
-        before = ((inner < outer) | (outer >= 128)).astype(jnp.bfloat16)
-        for block in range(count // 128):
-            part = labels[:, block * 128 : (block + 1) * 128]
-            member = lax.broadcasted_iota(jnp.int32, (devices, 128), 0) == part
-            sums = jnp.dot(
-                member.astype(jnp.bfloat16), before, preferred_element_type=jnp.float32
+def place_kernel(
+    rows_hbm, label_hbm, order_hbm, out_ref, position_ref, label_ref,
+    rows, order_ref, unit, digits, slots, pick, sems,
+):
+    count, width = rows.shape
+    devices = out_ref.shape[0]
+    half = width // 2
+    main_rows = devices * MAIN
+    copies = [
+        pltpu.make_async_copy(source, target, sems.at[k])
+        for k, (source, target) in enumerate(
+            ((label_hbm, label_ref), (order_hbm, order_ref), (rows_hbm, rows))
+        )
+    ]
+    for copy in copies:
+        copy.start()
+    for copy in copies:
+        copy.wait()
+
+    labels = label_ref[...]
+    carry = jnp.zeros((devices, 128), jnp.float32)
+    inner = lax.broadcasted_iota(jnp.int32, (128, 256), 0)
+    outer = lax.broadcasted_iota(jnp.int32, (128, 256), 1)
+    before = ((inner < outer) | (outer >= 128)).astype(jnp.bfloat16)
+    for block in range(count // 128):
+        at = slice(block * 128, (block + 1) * 128)
+        part = labels[:, at]
+        member = lax.broadcasted_iota(jnp.int32, (devices, 128), 0) == part
+        sums = jnp.dot(
+            member.astype(jnp.bfloat16), before, preferred_element_type=jnp.float32
+        )
+        rank = jnp.where(member, sums[:, :128] + carry, 0.0)
+        carry = carry + sums[:, 128:]
+        position = jnp.sum(rank, axis=0, keepdims=True).astype(jnp.int32)
+        position_ref[:, at] = position
+        slots[0:1, at] = jnp.where(position < MAIN, part * MAIN + position, -1)
+        slots[1:2, at] = jnp.where(position < MAIN, -1, part * TAIL + position - MAIN)
+
+    slot = slots[...]
+    main_at = lax.broadcasted_iota(jnp.int32, (main_rows, count), 0)
+    pick[:main_rows, :] = (main_at == slot[0:1]).astype(jnp.float32).astype(jnp.bfloat16)
+    tail_at = lax.broadcasted_iota(jnp.int32, (devices * TAIL, count), 0)
+    pick[main_rows:, :] = (tail_at == slot[1:2]).astype(jnp.float32).astype(jnp.bfloat16)
+
+    order = order_ref[...]
+    line = lax.broadcasted_iota(jnp.int32, (128, count), 0)
+    digit = jnp.where(
+        (line == 0) | (line == 4),
+        order >> 12,
+        jnp.where(
+            (line == 1) | (line == 5),
+            (order >> 6) & 63,
+            jnp.where(
+                (line == 2) | (line == 6),
+                order & 63,
+                jnp.where((line == 3) | (line == 7), 1, 0),
+            ),
+        ),
+    )
+    digits[...] = digit.astype(jnp.float32).astype(jnp.bfloat16)
+    for block in range(4):
+        at = slice(block * count // 4, (block + 1) * count // 4)
+        values = rows[at, :].astype(jnp.float32)
+        scale = lax.rsqrt(
+            jnp.mean(values * values, axis=1, keepdims=True) + 1e-06
+        ) * width ** (-0.5)
+        unit[at, :] = (values * scale).astype(jnp.bfloat16)
+
+    def upper(n):
+        return lax.broadcasted_iota(jnp.int32, (devices // 2, 8, n), 1) >= 4
+
+    main_digits = lax.dot_general(
+        pick[:main_rows, :], digits[...], NT, preferred_element_type=jnp.float32
+    ).reshape(devices // 2, 2, 8, 128)
+    tail_digits = lax.dot_general(
+        pick[main_rows:, :], digits[...], NT, preferred_element_type=jnp.float32
+    ).reshape(devices // 2, 8, 128)
+    left = lax.broadcasted_iota(jnp.int32, (devices // 2, 8, 128), 2) < 4
+    places = jnp.stack(
+        [
+            jnp.where(left, main_digits[:, 0], jnp.where(upper(128), 0.0, tail_digits)),
+            jnp.where(
+                left,
+                main_digits[:, 1],
+                jnp.where(upper(128), 0.0, pltpu.roll(tail_digits, 4, 1)),
+            ),
+        ],
+        axis=1,
+    )
+    out_ref[:, :, width + half :] = places.reshape(devices, 8, 128).astype(jnp.bfloat16)
+    step = 256
+    for n in range(half // step):
+        low_at = slice(n * step, (n + 1) * step)
+        high_at = slice(half + n * step, half + (n + 1) * step)
+        for at in (low_at, high_at):
+            main = jnp.dot(
+                pick[:main_rows, :], unit[:, at], preferred_element_type=jnp.float32
             )
-            rank = jnp.where(member, sums[:, :128] + carry, 0.0)
-            carry = carry + sums[:, 128:]
-            position = jnp.sum(rank, axis=0, keepdims=True).astype(jnp.int32)
-            position_ref[:, block * 128 : (block + 1) * 128] = position
-            slots[0:1, block * 128 : (block + 1) * 128] = jnp.where(
-                position < MAIN, part * MAIN + position, -1
-            )
-            slots[1:2, block * 128 : (block + 1) * 128] = jnp.where(
-                position < MAIN, -1, part * TAIL + position - MAIN
-            )
-        order = order_ref[...]
-        line = lax.broadcasted_iota(jnp.int32, (128, count), 0)
-        digit = jnp.where(
-            (line == 0) | (line == 4),
-            order >> 12,
-            jnp.where(
-                (line == 1) | (line == 5),
-                (order >> 6) & 63,
-                jnp.where(
-                    (line == 2) | (line == 6),
-                    order & 63,
-                    jnp.where((line == 3) | (line == 7), 1, 0),
-                ),
-            ),
-        )
-        digits[...] = digit.astype(jnp.float32).astype(jnp.bfloat16)
-        for block in range(count // 128):
-            values = rows_ref[block * 128 : (block + 1) * 128, :].astype(jnp.float32)
-            scale = lax.rsqrt(
-                jnp.mean(values * values, axis=1, keepdims=True) + 1e-06
-            ) * width ** (-0.5)
-            unit[block * 128 : (block + 1) * 128, :] = (values * scale).astype(jnp.bfloat16)
-
-    slot = slots[...]
-    main_rows, tail_rows = partners * MAIN, partners * TAIL
-    main_at = lax.broadcasted_iota(jnp.int32, (main_rows, count), 0) + step * main_rows
-    tail_at = lax.broadcasted_iota(jnp.int32, (tail_rows, count), 0) + step * tail_rows
-    main_pick = (main_at == slot[0:1]).astype(jnp.bfloat16)
-    tail_pick = (tail_at == slot[1:2]).astype(jnp.bfloat16)
-    main = jnp.dot(main_pick, unit[...], preferred_element_type=jnp.float32)
-    tail = jnp.dot(tail_pick, unit[...], preferred_element_type=jnp.float32)
-    main_digits = lax.dot_general(
-        main_pick, digits[...], NT, preferred_element_type=jnp.float32
-    )
-    tail_digits = lax.dot_general(
-        tail_pick, digits[...], NT, preferred_element_type=jnp.float32
-    )
-    half = width // 2
-    upper_half = lax.broadcasted_iota(jnp.int32, (8, half), 0) >= 4
-    upper_line = lax.broadcasted_iota(jnp.int32, (8, 128), 0) >= 4
-    left = lax.broadcasted_iota(jnp.int32, (8, 128), 1) < 4
-    for partner in range(partners):
-        out_ref[partner, :, :width] = main[partner * 8 : (partner + 1) * 8, :].astype(
-            jnp.bfloat16
-        )
-    for pair in range(partners // 2):
-        rows = tail[pair * 8 : (pair + 1) * 8, :]
-        first, second = fold_pair(rows[:, :half], rows[:, half:], upper_half)
-        out_ref[2 * pair, :, width : width + half] = first.astype(jnp.bfloat16)
-        out_ref[2 * pair + 1, :, width : width + half] = second.astype(jnp.bfloat16)
-        places = tail_digits[pair * 8 : (pair + 1) * 8, :]
-        for odd, tail_part in ((0, places), (1, pltpu.roll(places, 4, 0))):
-            partner = 2 * pair + odd
-            both = jnp.where(
-                left,
-                main_digits[partner * 8 : (partner + 1) * 8, :],
-                jnp.where(upper_line, 0.0, tail_part),
-            )
-            out_ref[partner, :, width + half :] = both.astype(jnp.bfloat16)
+            out_ref[:, :, at] = main.reshape(devices, 8, step).astype(jnp.bfloat16)
+        low, high = (
+            jnp.dot(
+                pick[main_rows:, :], unit[:, at], preferred_element_type=jnp.float32
+            ).reshape(devices // 2, 8, step)
+            for at in (low_at, high_at)
+        )
+        folded = jnp.stack(
+            [
+                jnp.where(upper(step), pltpu.roll(high, 4, 1), low),
+                jnp.where(upper(step), high, pltpu.roll(low, 4, 1)),
+            ],
+            axis=1,
+        )
+        out_ref[:, :, width + n * step : width + (n + 1) * step] = folded.reshape(
+            devices, 8, step
+        ).astype(jnp.bfloat16)
 
 
 def score_kernel(got_ref, best_ref, member, digits, earlier_col, row_best, col_best):
@@ -233,34 +254,33 @@
     devices = lax.axis_size("grp") * lax.axis_size("blk")
     total = width + width // 2 + 128
     docs = devices * (MAIN + TAIL)
-    label_row = labels.reshape(1, rows)
-    order_row = order_ids.reshape(1, rows)
-    partners = 16
     params = pltpu.CompilerParams(vmem_limit_bytes=VMEM_LIMIT)
-
-    def whole(*shape):
-        return pl.BlockSpec(shape, lambda *_: (0,) * len(shape))
-
-    outgoing, position = pl.pallas_call(
+    in_hbm = pl.BlockSpec(memory_space=pltpu.HBM)
+    outgoing, position, label_row = pl.pallas_call(
         place_kernel,
-        grid=(devices // partners,),
-        in_specs=[whole(rows, width), whole(1, rows), whole(1, rows)],
-        out_specs=[
-            pl.BlockSpec((partners, 8, total), lambda step: (step, 0, 0)),
-            whole(1, rows),
-        ],
+        in_specs=[in_hbm] * 3,
         out_shape=[
             jax.ShapeDtypeStruct((devices, 8, total), jnp.bfloat16),
+            jax.ShapeDtypeStruct((1, rows), jnp.int32),
             jax.ShapeDtypeStruct((1, rows), jnp.int32),
         ],
         scratch_shapes=[
             pltpu.VMEM((rows, width), jnp.bfloat16),
+            pltpu.VMEM((1, rows), jnp.int32),
+            pltpu.VMEM((rows, width), jnp.bfloat16),
             pltpu.VMEM((128, rows), jnp.bfloat16),
             pltpu.VMEM((8, rows), jnp.int32),
+            pltpu.VMEM((docs, rows), jnp.bfloat16),
+            pltpu.SemaphoreType.DMA((3,)),
         ],
         compiler_params=params,
         name="place",
-    )(embeddings, label_row, order_row)
+    )(
+        *(
+            pltpu.with_memory_space_constraint(x, pltpu.HBM)
+            for x in (embeddings, labels.reshape(1, rows), order_ids.reshape(1, rows))
+        )
+    )
     got = lax.all_to_all(outgoing, ("grp", "blk"), split_axis=0, concat_axis=0, tiled=True)
     best = pl.pallas_call(
         score_kernel,

time: 86.5 us -> 81.2 us (0.939)
  local copies, waits for them, and re-layouts: 2.97 us -> 0 us
  Pallas kernels: 13.3 us -> 11 us
    unnamed x8 -> x0, local copies, waits for them, and re-layouts: 2.97 us -> none
    pallas_call x1, Pallas kernels: 8.62 us -> 6.33 us  [shards(): pl.pallas_call(place_kernel, in_specs=[in_hbm] * 3, out_shape=[jax.ShapeD...]
where the time goes in v2:
time: 81.2 us; the launch traced here: 81 us
  blocking collectives  70 us (86%)
  Pallas kernels  11 us (14%)
    all_to_all x1, blocking collectives, shards(): lax.all_to_all(outgoing, ('grp', 'blk'), split_axis=0, concat_axis=0, til...  56.3 us
    all_to_all x1, blocking collectives, shards(): lax.all_to_all(best.reshape(devices, 1, 128), ('grp', 'blk'), split_axis=...  13.6 us
    pallas_call x1, Pallas kernels, shards(): pl.pallas_call(place_kernel, in_specs=[in_hbm] * 3, out_shape=[jax.ShapeD...  6.33 us
    pallas_call x1, Pallas kernels, shards(): pl.pallas_call(score_kernel, out_shape=jax.ShapeDtypeStruct((devices, 128...  3.83 us

profile of v2, /device:TPU:1, one launch (start us, length us, event | category | flops | bytes accessed | tf_op | source)
XLA Modules:
  0.0 81.0 jit_solution(13099611066254508552)
XLA Ops:
  0.0 6.3 %place.1 = (bf16[128,8,1664]{2,1,0:T(8,128)(2,1)S(1)}, s32[1,1024]{1,0:T(1,128)S(1)}, s32[1,1024]{1,0:T(1,128)S(1)}) custom-call(bf16[1024,1024]{1,0:T(8,128)(2,1)} %rows_hbm.1, s32[1,1024]{1,0:T(1,128)} %bitcast.9, s32[1,1024]{1,0:T(1,128)} %bitcast.10), custom_call_target="tpu_custom_call" | custom-call | tf_op jit(solution)/shard_map/place/pallas_call | solution.py:259
  6.3 56.3 %all_to_all.10.got_ref = bf16[128,8,1664]{2,1,0:T(8,128)(2,1)S(1)} all-to-all(bf16[128,8,1664]{2,1,0:T(8,128)(2,1)S(1)} %get-tuple-element.8), channel_id=1, replica_groups=mesh['grp'=32,'blk'=4] {'grp','blk'}, dimensions={0} | all-to-all | bytes 6815744 | tf_op jit(solution)/shard_map/all_to_all | solution.py:284
  62.7 3.8 %score.1 = f32[128,128]{1,0:T(8,128)S(1)} custom-call(bf16[128,8,1664]{2,1,0:T(8,128)(2,1)S(1)} %all_to_all.10.got_ref), custom_call_target="tpu_custom_call" | custom-call | tf_op jit(solution)/shard_map/score/pallas_call | solution.py:285
  66.5 13.6 %all_to_all.11 = f32[128,1,128]{2,1,0:T(1,128)S(1)} all-to-all(f32[128,1,128]{2,1,0:T(1,128)S(1)} %bitcast.7), channel_id=1, replica_groups=mesh['grp'=32,'blk'=4] {'grp','blk'}, dimensions={0} | all-to-all | bytes 131072 | tf_op jit(solution)/shard_map/all_to_all | solution.py:298
  80.1 0.9 %pick.1 = f32[1,1024]{1,0:T(1,128)} custom-call(f32[128,128]{1,0:T(8,128)S(1)} %bitcast.8, s32[1,1024]{1,0:T(1,128)S(1)} %get-tuple-element.9.label_ref, s32[1,1024]{1,0:T(1,128)S(1)} %get-tuple-element.10.position_ref), custom_call_target="tpu_custom_call" | custom-call | tf_op jit(solution)/shard_map/pick/pallas_call | solution.py:301

commit v3 on v2

v3 whole, which is shorter than its diff:
```python
import jax
import jax.numpy as jnp
from jax import lax
from jax.experimental import pallas as pl
from jax.experimental.pallas import tpu as pltpu
from jax.sharding import PartitionSpec as P

MAIN = 8
TAIL = 4
CAP = MAIN + TAIL
GROUP = 4
TURNS = (0, 2, 1, 3)
NT = (((1,), (1,)), ((), ()))
VMEM_LIMIT = 48 * 1024 * 1024


def place_kernel(
    rows_hbm, label_hbm, order_hbm, out_ref, position_ref, label_ref,
    rows, order_ref, unit, slots, pick, sems,
):
    count, width = rows.shape
    groups = out_ref.shape[0]
    devices = groups * GROUP
    half = width // 2
    main_rows, tail_rows = devices * MAIN, devices * TAIL
    parts = 4
    part_rows = count // parts
    small = [
        pltpu.make_async_copy(source, target, sems.at[parts + k])
        for k, (source, target) in enumerate(((label_hbm, label_ref), (order_hbm, order_ref)))
    ]
    large = []
    for k in range(parts):
        at = pl.ds(k * part_rows, part_rows)
        large.append(pltpu.make_async_copy(rows_hbm.at[at, :], rows.at[at, :], sems.at[k]))
    for copy in small + large:
        copy.start()
    for copy in small:
        copy.wait()

    labels = label_ref[...]
    carry = jnp.zeros((devices, 128), jnp.float32)
    inner = lax.broadcasted_iota(jnp.int32, (128, 256), 0)
    outer = lax.broadcasted_iota(jnp.int32, (128, 256), 1)
    before = ((inner < outer) | (outer >= 128)).astype(jnp.bfloat16)
    for block in range(count // 128):
        at = slice(block * 128, (block + 1) * 128)
        part = labels[:, at]
        member = lax.broadcasted_iota(jnp.int32, (devices, 128), 0) == part
        sums = jnp.dot(
            member.astype(jnp.bfloat16), before, preferred_element_type=jnp.float32
        )
        rank = jnp.where(member, sums[:, :128] + carry, 0.0)
        carry = carry + sums[:, 128:]
        position = jnp.sum(rank, axis=0, keepdims=True).astype(jnp.int32)
        position_ref[:, at] = position
        slots[0:1, at] = jnp.where(position < MAIN, part * MAIN + position, -1)
        slots[1:2, at] = jnp.where(position < MAIN, -1, part * TAIL + position - MAIN)
    for copy in large:
        copy.wait()

    slot = slots[...]
    main_pick = lax.broadcasted_iota(jnp.int32, (main_rows, count), 0) == slot[0:1]
    pick[:main_rows, :] = main_pick.astype(jnp.float32).astype(jnp.bfloat16)
    tail_pick = lax.broadcasted_iota(jnp.int32, (tail_rows, count), 0) == slot[1:2]
    pick[main_rows:, :] = tail_pick.astype(jnp.float32).astype(jnp.bfloat16)

    for k in range(parts):
        at = slice(k * part_rows, (k + 1) * part_rows)
        values = rows[at, :].astype(jnp.float32)
        scale = lax.rsqrt(
            jnp.mean(values * values, axis=1, keepdims=True) + 1e-06
        ) * width ** (-0.5)
        unit[at, :] = (values * scale).astype(jnp.bfloat16)

    key = (order_ref[...] + 262144).astype(jnp.float32)

    def digits(chosen, row):
        found = jnp.where(
            lax.broadcasted_iota(jnp.int32, (chosen, count), 0) == row,
            jnp.broadcast_to(key, (chosen, count)),
            0.0,
        )
        total = found[:, :128]
        for block in range(1, count // 128):
            total = total + found[:, block * 128 : (block + 1) * 128]
        total = jnp.sum(total, axis=1, keepdims=True).astype(jnp.int32)
        total = jnp.broadcast_to(total, (chosen, 128))
        digit = lax.broadcasted_iota(jnp.int32, (chosen, 128), 1) & 3
        shift = jnp.where(
            digit == 0, 12, jnp.where(digit == 1, 6, jnp.where(digit == 2, 0, 18))
        )
        return ((total >> shift) & 63).astype(jnp.float32)

    line = lax.broadcasted_iota(jnp.int32, (1, 8, 128), 1)
    owner = lax.broadcasted_iota(jnp.int32, (1, 8, 128), 2) >> 2
    main_digits = digits(main_rows, slot[0:1]).reshape(devices, 8, 128)
    places = jnp.sum(jnp.where(owner == line, main_digits, 0.0), axis=1, keepdims=True)
    tail_digits = digits(tail_rows, slot[1:2]).reshape(devices // 2, 8, 128)
    mine = owner == (line & 3) + MAIN
    tail_places = jnp.stack(
        [
            jnp.sum(jnp.where(mine & (line < 4), tail_digits, 0.0), axis=1, keepdims=True),
            jnp.sum(jnp.where(mine & (line >= 4), tail_digits, 0.0), axis=1, keepdims=True),
        ],
        axis=1,
    ).reshape(devices, 1, 128)
    places = jnp.broadcast_to(places + tail_places, (devices, 8, 128))
    places = places.reshape(groups, GROUP, 8, 128)

    def put(tile, values):
        values = values.reshape(groups, GROUP, 8, 128)
        if tile:
            for e in range(GROUP):
                out_ref[:, CAP * e + tile] = values[:, e].astype(jnp.bfloat16)
            return
        out_ref[:, 0] = values[:, 0].astype(jnp.bfloat16)
        turn = line >> 1
        for e in range(1, GROUP + 1):
            mixed = jnp.where(turn == e - 1, places[:, e - 1], values[:, e - 1])
            if e < GROUP:
                mixed = jnp.where(turn >= e, values[:, e], mixed)
            out_ref[:, CAP * e] = mixed.astype(jnp.bfloat16)

    step = 256
    upper = lax.broadcasted_iota(jnp.int32, (devices // 2, 8, step), 1) >= 4
    for n in range(half // step):
        ends = (n * step, half + n * step)
        for first in ends:
            main = jnp.dot(
                pick[:main_rows, :],
                unit[:, first : first + step],
                preferred_element_type=jnp.float32,
            )
            for k in range(step // 128):
                put(first // 128 + k, main[:, k * 128 : (k + 1) * 128])
        low, high = (
            jnp.dot(
                pick[main_rows:, :],
                unit[:, first : first + step],
                preferred_element_type=jnp.float32,
            ).reshape(devices // 2, 8, step)
            for first in ends
        )
        folded = jnp.stack(
            [
                jnp.where(upper, pltpu.roll(high, 4, 1), low),
                jnp.where(upper, high, pltpu.roll(low, 4, 1)),
            ],
            axis=1,
        ).reshape(devices, 8, step)
        for k in range(step // 128):
            put(MAIN + n * step // 128 + k, folded[:, :, k * 128 : (k + 1) * 128])


def score_kernel(got_ref, best_ref, member, digits, column, row_best, col_best, results):
    groups = got_ref.shape[0]
    devices = groups * GROUP
    docs, width = member.shape
    pieces = width // 128
    main_rows = devices * MAIN
    last = GROUP * CAP
    me = lax.axis_index("blk")
    line = lax.broadcasted_iota(jnp.int32, (8, 128), 0)
    lane = lax.broadcasted_iota(jnp.int32, (8, 128), 1)
    turn, owner = line >> 1, lane >> 2
    inner = (turn == 1) | (turn == 2)
    first_half = turn < 2

    def both(a, b):
        return jnp.concatenate([a, b], axis=0).astype(jnp.bfloat16)

    for group in range(groups):
        chunks = []
        for turns in range(GROUP):
            source = (me + turns) & 3
            base = CAP * source - jnp.where(source < me, 1, 0)
            tiles = [
                got_ref[group, jnp.clip(base + t, 0, last)].astype(jnp.float32)
                for t in range(CAP + 2)
            ]
            if turns:
                tiles = [
                    jnp.where(turn >= turns, tiles[t], tiles[t + 1]) for t in range(CAP + 1)
                ]
            tiles[0] = jnp.where(((turn - turns) & 3) >= me, tiles[0], tiles[CAP])
            chunks.append(tiles)
        places = got_ref[group, last].astype(jnp.float32)
        for e in range(GROUP - 1):
            places = jnp.where(
                turn == e, got_ref[group, CAP * (e + 1)].astype(jnp.float32), places
            )
        places = pltpu.roll(places, (8 - 2 * me) & 7, 0)
        places = [
            jnp.broadcast_to(places[2 * turns : 2 * turns + 1, :], (8, 128))
            for turns in range(GROUP)
        ]
        for k in range(2):
            a, b = TURNS[2 * k], TURNS[2 * k + 1]
            at = slice(group * 32 + k * 16, group * 32 + k * 16 + 16)
            for t in range(pieces):
                member[at, t * 128 : (t + 1) * 128] = both(chunks[a][t], chunks[b][t])
            digits[at, :] = both(
                *(
                    jnp.where(owner == ((line - 2 * turns) & 7), places[turns], 0.0)
                    for turns in (a, b)
                )
            )
        at = slice(main_rows + group * 16, main_rows + group * 16 + 16)
        for t in range(pieces // 2):
            a, b, c, d = (chunks[turns][MAIN + t] for turns in range(GROUP))
            member[at, t * 128 : (t + 1) * 128] = both(
                jnp.where(first_half, a, c), jnp.where(inner, b, d)
            )
            t = t + pieces // 2
            member[at, t * 128 : (t + 1) * 128] = both(
                pltpu.roll(jnp.where(first_half, c, a), 4, 0),
                pltpu.roll(jnp.where(inner, d, b), 4, 0),
            )
        digits[at, :] = both(
            jnp.where(
                owner == MAIN + (line & 3), jnp.where(first_half, places[0], places[2]), 0.0
            ),
            jnp.where(
                owner == MAIN + ((line - 2) & 3), jnp.where(inner, places[1], places[3]), 0.0
            ),
        )

    def weights(shape, axis):
        at = lax.broadcasted_iota(jnp.int32, shape, axis)
        digit = at & 3
        weight = jnp.where(
            digit == 0,
            4096.0,
            jnp.where(digit == 1, 64.0, jnp.where(digit == 2, 1.0, -262144.0)),
        )
        return jnp.where(at < 4 * CAP, weight, 0.0).astype(jnp.bfloat16)

    column[...] = jnp.dot(
        digits[...], weights((128, 128), 0), preferred_element_type=jnp.float32
    )
    place_row = lax.dot_general(
        weights((8, 128), 1), digits[...], NT, preferred_element_type=jnp.float32
    )
    step = 256
    col_best[...] = jnp.full_like(col_best, -1.0)
    for i in range(docs // step):
        mine = slice(i * step, (i + 1) * step)
        best = jnp.full((step, 128), -1.0, jnp.float32)
        for j in range(i + 1):
            theirs = slice(j * step, (j + 1) * step)
            scores = lax.dot_general(
                member[mine, :], member[theirs, :], NT, preferred_element_type=jnp.float32
            )
            for k in range(step // 128):
                at = j * step + k * 128
                part = scores[:, k * 128 : (k + 1) * 128]
                earlier = place_row[0:1, at : at + 128] < column[mine, :]
                best = jnp.maximum(best, jnp.where(earlier, part, -1.0))
                if j != i:
                    other = jnp.where(earlier, -1.0, part)
                    col_best[:, at : at + 128] = jnp.maximum(
                        col_best[:, at : at + 128],
                        jnp.max(other.reshape(step // 8, 8, 128), axis=0),
                    )
        row_best[mine, :] = jnp.broadcast_to(
            jnp.max(best, axis=1, keepdims=True), (step, 128)
        )

    line = lax.broadcasted_iota(jnp.int32, (128, 128), 0)
    lane = lax.broadcasted_iota(jnp.int32, (128, 128), 1)
    for block in range(docs // 128):
        at = block * 128
        best = jnp.maximum(
            row_best[at : at + 128, :],
            jnp.broadcast_to(
                jnp.max(col_best[:, at : at + 128].T, axis=1, keepdims=True), (128, 128)
            ),
        )
        if at < main_rows:
            index = (line >> 3) & 3
            turns = jnp.where(index == 1, 2, jnp.where(index == 2, 1, index))
            kept = jnp.where(lane == ((line - 2 * turns) & 7), best, -2.0)
            results[block * 16 : (block + 1) * 16, :] = jnp.max(
                kept.reshape(16, 8, 128), axis=1
            )
        else:
            odd = ((line >> 3) & 1) * 2
            kept = jnp.where(lane == MAIN + ((line - odd) & 3), best, -2.0)
            kept = kept.reshape(8, 2, 8, 128)
            row = lax.broadcasted_iota(jnp.int32, (8, 8, 128), 1)
            first = (at - main_rows) // TAIL
            for index in range(GROUP):
                start = (0, 4, 2, 6)[index]
                mine = ((row - start) & 7) < 4
                found = jnp.max(jnp.where(mine, kept[:, index // 2], -2.0), axis=1)
                where = pl.ds(first + index, 8, stride=GROUP)
                results[where, :] = jnp.maximum(results[where, :], found)
    for index, turns in enumerate(TURNS):
        best_ref[pl.ds((me + turns) & 3, groups, stride=GROUP), :] = results[
            pl.ds(index, groups, stride=GROUP), :
        ]


def pick_kernel(got_ref, label_ref, position_ref, out_ref):
    devices = got_ref.shape[0]
    count = label_ref.shape[1]
    table = got_ref[...].T[:16, :]
    top = table.astype(jnp.bfloat16)
    rest = table - top.astype(jnp.float32)
    middle = rest.astype(jnp.bfloat16)
    low = (rest - middle.astype(jnp.float32)).astype(jnp.bfloat16)
    pick = (
        lax.broadcasted_iota(jnp.int32, (devices, count), 0) == label_ref[...]
    ).astype(jnp.bfloat16)

    def dot(part):
        return jnp.dot(part, pick, preferred_element_type=jnp.float32)

    values = (dot(top) + dot(middle)) + dot(low)
    line = lax.broadcasted_iota(jnp.int32, (16, count), 0)
    out_ref[...] = jnp.sum(
        jnp.where(line == position_ref[...], values, 0.0), axis=0, keepdims=True
    )


def shards(embeddings, labels, order_ids):
    rows, width = embeddings.shape
    devices = lax.axis_size("grp") * lax.axis_size("blk")
    groups, units = devices // GROUP, GROUP * CAP + 1
    docs = devices * CAP
    params = pltpu.CompilerParams(vmem_limit_bytes=VMEM_LIMIT)
    in_hbm = pl.BlockSpec(memory_space=pltpu.HBM)
    outgoing, position, label_row = pl.pallas_call(
        place_kernel,
        in_specs=[in_hbm] * 3,
        out_shape=[
            jax.ShapeDtypeStruct((groups, units, 8, 128), jnp.bfloat16),
            jax.ShapeDtypeStruct((1, rows), jnp.int32),
            jax.ShapeDtypeStruct((1, rows), jnp.int32),
        ],
        scratch_shapes=[
            pltpu.VMEM((rows, width), jnp.bfloat16),
            pltpu.VMEM((1, rows), jnp.int32),
            pltpu.VMEM((rows, width), jnp.bfloat16),
            pltpu.VMEM((8, rows), jnp.int32),
            pltpu.VMEM((docs, rows), jnp.bfloat16),
            pltpu.SemaphoreType.DMA((6,)),
        ],
        compiler_params=params,
        name="place",
    )(
        *(
            pltpu.with_memory_space_constraint(x, pltpu.HBM)
            for x in (embeddings, labels.reshape(1, rows), order_ids.reshape(1, rows))
        )
    )
    got = lax.all_to_all(
        outgoing.reshape(devices, units, 2, 128),
        ("grp", "blk"),
        split_axis=0,
        concat_axis=0,
        tiled=True,
    )
    best = pl.pallas_call(
        score_kernel,
        out_shape=jax.ShapeDtypeStruct((devices, 128), jnp.float32),
        scratch_shapes=[
            pltpu.VMEM((docs, width), jnp.bfloat16),
            pltpu.VMEM((docs, 128), jnp.bfloat16),
            pltpu.VMEM((docs, 128), jnp.float32),
            pltpu.VMEM((docs, 128), jnp.float32),
            pltpu.VMEM((8, docs), jnp.float32),
            pltpu.VMEM((devices, 128), jnp.float32),
        ],
        compiler_params=params,
        name="score",
    )(got.reshape(groups, units, 8, 128))
    returned = lax.all_to_all(
        best.reshape(devices, 1, 128), ("grp", "blk"), split_axis=0, concat_axis=0, tiled=True
    ).reshape(devices, 128)
    picked = pl.pallas_call(
        pick_kernel,
        out_shape=jax.ShapeDtypeStruct((1, rows), jnp.float32),
        compiler_params=params,
        name="pick",
    )(returned, label_row, position)
    return picked.reshape(rows)


def solution(mesh):
    placed = (P(("grp", "blk"), None), P(("grp", "blk"), None), P(("grp", "blk")))
    return jax.shard_map(
        shards, mesh=mesh, in_specs=placed, out_specs=P(("grp", "blk")), check_vma=False
    )
```

time: 81.2 us -> 79.5 us (0.979)
  blocking collectives: 70 us -> 67.8 us
    all_to_all x1, blocking collectives: 56.3 us -> 54.2 us  [shards(): lax.all_to_all(outgoing.reshape(devices, units, 2, 128), ('grp', 'blk'),...]
where the time goes in v3:
time: 79.5 us; the launch traced here: 79.4 us
  blocking collectives  67.8 us (85%)
  Pallas kernels  11.6 us (15%)
    all_to_all x1, blocking collectives, shards(): lax.all_to_all(outgoing.reshape(devices, units, 2, 128), ('grp', 'blk'),...  54.2 us
    all_to_all x1, blocking collectives, shards(): lax.all_to_all(best.reshape(devices, 1, 128), ('grp', 'blk'), split_axis=...  13.5 us
    pallas_call x1, Pallas kernels, shards(): pl.pallas_call(place_kernel, in_specs=[in_hbm] * 3, out_shape=[jax.ShapeD...  6.4 us
    pallas_call x1, Pallas kernels, shards(): pl.pallas_call(score_kernel, out_shape=jax.ShapeDtypeStruct((devices, 128...  4.3 us

profile of v3, /device:TPU:1, one launch (start us, length us, event | category | flops | bytes accessed | tf_op | source)
XLA Modules:
  0.0 79.4 jit_solution(14341038098776058155)
XLA Ops:
  0.0 6.4 %place.1 = (bf16[32,49,8,128]{3,2,1,0:T(8,128)(2,1)S(1)}, s32[1,1024]{1,0:T(1,128)S(1)}, s32[1,1024]{1,0:T(1,128)S(1)}) custom-call(bf16[1024,1024]{1,0:T(8,128)(2,1)} %rows_hbm.1, s32[1,1024]{1,0:T(1,128)} %bitcast.13, s32[1,1024]{1,0:T(1,128)} %bitcast.14), custom_call_target="tpu_custom_call" | custom-call | tf_op jit(solution)/shard_map/place/pallas_call | solution.py:334
  6.4 54.2 %all_to_all.10 = bf16[128,49,2,128]{3,2,1,0:T(2,128)(2,1)S(1)} all-to-all(bf16[128,49,2,128]{3,2,1,0:T(2,128)(2,1)S(1)} %bitcast.10), channel_id=1, replica_groups=mesh['grp'=32,'blk'=4] {'grp','blk'}, dimensions={0} | all-to-all | bytes 6422528 | tf_op jit(solution)/shard_map/all_to_all | solution.py:358
  60.6 4.3 %score.1 = f32[128,128]{1,0:T(8,128)S(1)} custom-call(bf16[32,49,8,128]{3,2,1,0:T(8,128)(2,1)S(1)} %bitcast.9), custom_call_target="tpu_custom_call" | custom-call | tf_op jit(solution)/shard_map/score/pallas_call | solution.py:365
  65.0 13.5 %all_to_all.11 = f32[128,1,128]{2,1,0:T(1,128)S(1)} all-to-all(f32[128,1,128]{2,1,0:T(1,128)S(1)} %bitcast.11), channel_id=1, replica_groups=mesh['grp'=32,'blk'=4] {'grp','blk'}, dimensions={0} | all-to-all | bytes 131072 | tf_op jit(solution)/shard_map/all_to_all | solution.py:379
  78.5 0.9 %pick.1 = f32[1,1024]{1,0:T(1,128)} custom-call(f32[128,128]{1,0:T(8,128)S(1)} %bitcast.12, s32[1,1024]{1,0:T(1,128)S(1)} %get-tuple-element.9.label_ref, s32[1,1024]{1,0:T(1,128)S(1)} %get-tuple-element.10.position_ref), custom_call_target="tpu_custom_call" | custom-call | tf_op jit(solution)/shard_map/pick/pallas_call | solution.py:382

commit v4 on v3

--- a/solution.py
+++ b/solution.py
@@ -15,8 +15,8 @@
 
 
 def place_kernel(
-    rows_hbm, label_hbm, order_hbm, out_ref, position_ref, label_ref,
-    rows, order_ref, unit, slots, pick, sems,
+    rows_hbm, label_hbm, order_hbm, out_ref, lane_ref, label_ref,
+    rows, order_ref, unit, pick, members, marks, places, sems,
 ):
     count, width = rows.shape
     groups = out_ref.shape[0]
@@ -25,7 +25,7 @@
     main_rows, tail_rows = devices * MAIN, devices * TAIL
     parts = 4
     part_rows = count // parts
-    small = [
+    copies = [
         pltpu.make_async_copy(source, target, sems.at[parts + k])
         for k, (source, target) in enumerate(((label_hbm, label_ref), (order_hbm, order_ref)))
     ]
@@ -33,37 +33,71 @@
     for k in range(parts):
         at = pl.ds(k * part_rows, part_rows)
         large.append(pltpu.make_async_copy(rows_hbm.at[at, :], rows.at[at, :], sems.at[k]))
-    for copy in small + large:
+    for copy in copies + large:
         copy.start()
-    for copy in small:
+    for copy in copies:
         copy.wait()
 
+    me = lax.axis_index("blk")
     labels = label_ref[...]
     carry = jnp.zeros((devices, 128), jnp.float32)
     inner = lax.broadcasted_iota(jnp.int32, (128, 256), 0)
     outer = lax.broadcasted_iota(jnp.int32, (128, 256), 1)
     before = ((inner < outer) | (outer >= 128)).astype(jnp.bfloat16)
+    slot_of = lax.broadcasted_iota(jnp.int32, (128, 128), 0) >> 2
+    digit_of = lax.broadcasted_iota(jnp.int32, (128, 128), 0) & 3
+    shift = jnp.where(
+        digit_of == 0, 12, jnp.where(digit_of == 1, 6, jnp.where(digit_of == 2, 0, 18))
+    )
+    positions = []
     for block in range(count // 128):
         at = slice(block * 128, (block + 1) * 128)
         part = labels[:, at]
         member = lax.broadcasted_iota(jnp.int32, (devices, 128), 0) == part
-        sums = jnp.dot(
-            member.astype(jnp.bfloat16), before, preferred_element_type=jnp.float32
-        )
+        ones = member.astype(jnp.float32).astype(jnp.bfloat16)
+        members[:, at] = ones
+        sums = jnp.dot(ones, before, preferred_element_type=jnp.float32)
         rank = jnp.where(member, sums[:, :128] + carry, 0.0)
         carry = carry + sums[:, 128:]
         position = jnp.sum(rank, axis=0, keepdims=True).astype(jnp.int32)
-        position_ref[:, at] = position
-        slots[0:1, at] = jnp.where(position < MAIN, part * MAIN + position, -1)
-        slots[1:2, at] = jnp.where(position < MAIN, -1, part * TAIL + position - MAIN)
+        positions.append(position)
+        turned = (position + 2 * ((me - part) & 3)) & 7
+        lane_ref[:, at] = jnp.where(position < MAIN, turned, MAIN + turned)
+        digit = ((order_ref[:, at] + 262144) >> shift) & 63
+        marks[:, at] = (
+            jnp.where(slot_of == position, digit, 0).astype(jnp.float32).astype(jnp.bfloat16)
+        )
     for copy in large:
         copy.wait()
 
-    slot = slots[...]
-    main_pick = lax.broadcasted_iota(jnp.int32, (main_rows, count), 0) == slot[0:1]
-    pick[:main_rows, :] = main_pick.astype(jnp.float32).astype(jnp.bfloat16)
-    tail_pick = lax.broadcasted_iota(jnp.int32, (tail_rows, count), 0) == slot[1:2]
-    pick[main_rows:, :] = tail_pick.astype(jnp.float32).astype(jnp.bfloat16)
+    position = jnp.concatenate(positions, axis=1)
+    index = lax.broadcasted_iota(jnp.int32, (128, 128), 0).astype(jnp.float32)
+    index = jnp.concatenate([index.astype(jnp.bfloat16)] * (count // 128), axis=1)
+    index = index.reshape(8, 16, count)
+    one, zero = jnp.ones((), jnp.bfloat16), jnp.zeros((), jnp.bfloat16)
+
+    def choose(first, chosen, code):
+        code = jnp.where(chosen, code, -1).astype(jnp.float32)
+        code = jnp.broadcast_to(code, (16, count)).astype(jnp.bfloat16)
+        pick[first : first + 128, :] = jnp.where(index == code[None], one, zero).reshape(
+            128, count
+        )
+
+    for block in range(main_rows // 128):
+        choose(
+            block * 128,
+            ((labels >> 4) == block) & (position < MAIN),
+            (labels & 15) * MAIN + position,
+        )
+    for block in range(tail_rows // 128):
+        choose(
+            main_rows + block * 128,
+            ((labels >> 5) == block) & (position >= MAIN),
+            (labels & 31) * TAIL + position - MAIN,
+        )
+    places[...] = lax.dot_general(
+        members[...], marks[...], NT, preferred_element_type=jnp.float32
+    )
 
     for k in range(parts):
         at = slice(k * part_rows, (k + 1) * part_rows)
@@ -73,40 +107,7 @@
         ) * width ** (-0.5)
         unit[at, :] = (values * scale).astype(jnp.bfloat16)
 
-    key = (order_ref[...] + 262144).astype(jnp.float32)
-
-    def digits(chosen, row):
-        found = jnp.where(
-            lax.broadcasted_iota(jnp.int32, (chosen, count), 0) == row,
-            jnp.broadcast_to(key, (chosen, count)),
-            0.0,
-        )
-        total = found[:, :128]
-        for block in range(1, count // 128):
-            total = total + found[:, block * 128 : (block + 1) * 128]
-        total = jnp.sum(total, axis=1, keepdims=True).astype(jnp.int32)
-        total = jnp.broadcast_to(total, (chosen, 128))
-        digit = lax.broadcasted_iota(jnp.int32, (chosen, 128), 1) & 3
-        shift = jnp.where(
-            digit == 0, 12, jnp.where(digit == 1, 6, jnp.where(digit == 2, 0, 18))
-        )
-        return ((total >> shift) & 63).astype(jnp.float32)
-
-    line = lax.broadcasted_iota(jnp.int32, (1, 8, 128), 1)
-    owner = lax.broadcasted_iota(jnp.int32, (1, 8, 128), 2) >> 2
-    main_digits = digits(main_rows, slot[0:1]).reshape(devices, 8, 128)
-    places = jnp.sum(jnp.where(owner == line, main_digits, 0.0), axis=1, keepdims=True)
-    tail_digits = digits(tail_rows, slot[1:2]).reshape(devices // 2, 8, 128)
-    mine = owner == (line & 3) + MAIN
-    tail_places = jnp.stack(
-        [
-            jnp.sum(jnp.where(mine & (line < 4), tail_digits, 0.0), axis=1, keepdims=True),
-            jnp.sum(jnp.where(mine & (line >= 4), tail_digits, 0.0), axis=1, keepdims=True),
-        ],
-        axis=1,
-    ).reshape(devices, 1, 128)
-    places = jnp.broadcast_to(places + tail_places, (devices, 8, 128))
-    places = places.reshape(groups, GROUP, 8, 128)
+    turn = lax.broadcasted_iota(jnp.int32, (8, 128), 0) >> 1
 
     def put(tile, values):
         values = values.reshape(groups, GROUP, 8, 128)
@@ -114,13 +115,18 @@
             for e in range(GROUP):
                 out_ref[:, CAP * e + tile] = values[:, e].astype(jnp.bfloat16)
             return
-        out_ref[:, 0] = values[:, 0].astype(jnp.bfloat16)
-        turn = line >> 1
-        for e in range(1, GROUP + 1):
-            mixed = jnp.where(turn == e - 1, places[:, e - 1], values[:, e - 1])
-            if e < GROUP:
-                mixed = jnp.where(turn >= e, values[:, e], mixed)
-            out_ref[:, CAP * e] = mixed.astype(jnp.bfloat16)
+        for group in range(groups):
+            out_ref[group, 0] = values[group, 0].astype(jnp.bfloat16)
+            for e in range(1, GROUP + 1):
+                at = group * GROUP + e - 1
+                mixed = jnp.where(
+                    turn == e - 1,
+                    jnp.broadcast_to(places[at : at + 1, :], (8, 128)),
+                    values[group, e - 1],
+                )
+                if e < GROUP:
+                    mixed = jnp.where(turn >= e, values[group, e], mixed)
+                out_ref[group, CAP * e] = mixed.astype(jnp.bfloat16)
 
     step = 256
     upper = lax.broadcasted_iota(jnp.int32, (devices // 2, 8, step), 1) >= 4
@@ -263,64 +269,53 @@
                         col_best[:, at : at + 128],
                         jnp.max(other.reshape(step // 8, 8, 128), axis=0),
                     )
-        row_best[mine, :] = jnp.broadcast_to(
-            jnp.max(best, axis=1, keepdims=True), (step, 128)
-        )
-
-    line = lax.broadcasted_iota(jnp.int32, (128, 128), 0)
-    lane = lax.broadcasted_iota(jnp.int32, (128, 128), 1)
+        best = jnp.broadcast_to(jnp.max(best, axis=1, keepdims=True), (step, 128))
+        place = lax.broadcasted_iota(jnp.int32, (step, 128), 0) & 7
+        if i * step >= main_rows:
+            place = place + MAIN
+        best = jnp.where(lax.broadcasted_iota(jnp.int32, (step, 128), 1) == place, best, -2.0)
+        row_best[i * step // 8 : (i + 1) * step // 8, :] = jnp.max(
+            best.reshape(step // 8, 8, 128), axis=1
+        )
+
+    own = (
+        lax.broadcasted_iota(jnp.int32, (16, 128), 1) >> 3
+        == lax.broadcasted_iota(jnp.int32, (16, 128), 0)
+    )
     for block in range(docs // 128):
-        at = block * 128
-        best = jnp.maximum(
-            row_best[at : at + 128, :],
-            jnp.broadcast_to(
-                jnp.max(col_best[:, at : at + 128].T, axis=1, keepdims=True), (128, 128)
-            ),
-        )
-        if at < main_rows:
-            index = (line >> 3) & 3
-            turns = jnp.where(index == 1, 2, jnp.where(index == 2, 1, index))
-            kept = jnp.where(lane == ((line - 2 * turns) & 7), best, -2.0)
-            results[block * 16 : (block + 1) * 16, :] = jnp.max(
-                kept.reshape(16, 8, 128), axis=1
-            )
-        else:
-            odd = ((line >> 3) & 1) * 2
-            kept = jnp.where(lane == MAIN + ((line - odd) & 3), best, -2.0)
-            kept = kept.reshape(8, 2, 8, 128)
-            row = lax.broadcasted_iota(jnp.int32, (8, 8, 128), 1)
-            first = (at - main_rows) // TAIL
-            for index in range(GROUP):
-                start = (0, 4, 2, 6)[index]
-                mine = ((row - start) & 7) < 4
-                found = jnp.max(jnp.where(mine, kept[:, index // 2], -2.0), axis=1)
-                where = pl.ds(first + index, 8, stride=GROUP)
-                results[where, :] = jnp.maximum(results[where, :], found)
+        best = jnp.max(col_best[:, block * 128 : (block + 1) * 128], axis=0, keepdims=True)
+        best = jnp.where(own, jnp.broadcast_to(best, (16, 128)), -2.0)
+        for shift in (64, 32, 16, 8):
+            best = jnp.maximum(best, pltpu.roll(best, shift, 1))
+        at = slice(block * 16, (block + 1) * 16)
+        results[at, :] = jnp.maximum(best, row_best[at, :])
+    lane = lax.broadcasted_iota(jnp.int32, (groups, 128), 1)
     for index, turns in enumerate(TURNS):
-        best_ref[pl.ds((me + turns) & 3, groups, stride=GROUP), :] = results[
-            pl.ds(index, groups, stride=GROUP), :
-        ]
-
-
-def pick_kernel(got_ref, label_ref, position_ref, out_ref):
+        best_ref[pl.ds((me + turns) & 3, groups, stride=GROUP), :] = jnp.where(
+            lane < MAIN,
+            results[pl.ds(index, groups, stride=GROUP), :],
+            results[pl.ds(devices + index // 2, groups, stride=2), :],
+        )
+
+
+def pick_kernel(got_ref, label_ref, lane_ref, out_ref):
     devices = got_ref.shape[0]
     count = label_ref.shape[1]
-    table = got_ref[...].T[:16, :]
-    top = table.astype(jnp.bfloat16)
-    rest = table - top.astype(jnp.float32)
-    middle = rest.astype(jnp.bfloat16)
-    low = (rest - middle.astype(jnp.float32)).astype(jnp.bfloat16)
-    pick = (
-        lax.broadcasted_iota(jnp.int32, (devices, count), 0) == label_ref[...]
-    ).astype(jnp.bfloat16)
-
-    def dot(part):
-        return jnp.dot(part, pick, preferred_element_type=jnp.float32)
-
-    values = (dot(top) + dot(middle)) + dot(low)
-    line = lax.broadcasted_iota(jnp.int32, (16, count), 0)
+    table = got_ref[...].T[: 2 * MAIN, :]
+    top = table.astype(jnp.bfloat16).astype(jnp.float32)
+    rest = table - top
+    middle = rest.astype(jnp.bfloat16).astype(jnp.float32)
+    parts = jnp.concatenate([top, middle, rest - middle], axis=0).astype(jnp.bfloat16)
+    chosen = lax.broadcasted_iota(jnp.int32, (devices, count), 0) == label_ref[...]
+    values = jnp.dot(
+        parts,
+        chosen.astype(jnp.float32).astype(jnp.bfloat16),
+        preferred_element_type=jnp.float32,
+    )
+    values = (values[: 2 * MAIN] + values[2 * MAIN : 4 * MAIN]) + values[4 * MAIN :]
+    line = lax.broadcasted_iota(jnp.int32, (2 * MAIN, count), 0)
     out_ref[...] = jnp.sum(
-        jnp.where(line == position_ref[...], values, 0.0), axis=0, keepdims=True
+        jnp.where(line == lane_ref[...], values, 0.0), axis=0, keepdims=True
     )
 
 
@@ -331,7 +326,7 @@
     docs = devices * CAP
     params = pltpu.CompilerParams(vmem_limit_bytes=VMEM_LIMIT)
     in_hbm = pl.BlockSpec(memory_space=pltpu.HBM)
-    outgoing, position, label_row = pl.pallas_call(
+    outgoing, lane_row, label_row = pl.pallas_call(
         place_kernel,
         in_specs=[in_hbm] * 3,
         out_shape=[
@@ -343,8 +338,10 @@
             pltpu.VMEM((rows, width), jnp.bfloat16),
             pltpu.VMEM((1, rows), jnp.int32),
             pltpu.VMEM((rows, width), jnp.bfloat16),
-            pltpu.VMEM((8, rows), jnp.int32),
             pltpu.VMEM((docs, rows), jnp.bfloat16),
+            pltpu.VMEM((devices, rows), jnp.bfloat16),
+            pltpu.VMEM((128, rows), jnp.bfloat16),
+            pltpu.VMEM((devices, 128), jnp.float32),
             pltpu.SemaphoreType.DMA((6,)),
         ],
         compiler_params=params,
@@ -369,9 +366,9 @@
             pltpu.VMEM((docs, width), jnp.bfloat16),
             pltpu.VMEM((docs, 128), jnp.bfloat16),
             pltpu.VMEM((docs, 128), jnp.float32),
-            pltpu.VMEM((docs, 128), jnp.float32),
+            pltpu.VMEM((docs // 8, 128), jnp.float32),
             pltpu.VMEM((8, docs), jnp.float32),
-            pltpu.VMEM((devices, 128), jnp.float32),
+            pltpu.VMEM((docs // 8, 128), jnp.float32),
         ],
         compiler_params=params,
         name="score",
@@ -384,7 +381,7 @@
         out_shape=jax.ShapeDtypeStruct((1, rows), jnp.float32),
         compiler_params=params,
         name="pick",
-    )(returned, label_row, position)
+    )(returned, label_row, lane_row)
     return picked.reshape(rows)
 
 

time: 79.5 us -> 78.2 us (0.984)
  Pallas kernels: 11.6 us -> 10.3 us
    pallas_call x1, Pallas kernels: 6.4 us -> 5.27 us  [shards(): pl.pallas_call(place_kernel, in_specs=[in_hbm] * 3, out_shape=[jax.ShapeD...]
where the time goes in v4:
time: 78.2 us; the launch traced here: 78 us
  blocking collectives  67.7 us (87%)
  Pallas kernels  10.3 us (13%)
    all_to_all x1, blocking collectives, shards(): lax.all_to_all(outgoing.reshape(devices, units, 2, 128), ('grp', 'blk'),...  54.2 us
    all_to_all x1, blocking collectives, shards(): lax.all_to_all(best.reshape(devices, 1, 128), ('grp', 'blk'), split_axis=...  13.5 us
    pallas_call x1, Pallas kernels, shards(): pl.pallas_call(place_kernel, in_specs=[in_hbm] * 3, out_shape=[jax.ShapeD...  5.27 us
    pallas_call x1, Pallas kernels, shards(): pl.pallas_call(score_kernel, out_shape=jax.ShapeDtypeStruct((devices, 128...  4.15 us

profile of v4, /device:TPU:1, one launch (start us, length us, event | category | flops | bytes accessed | tf_op | source)
XLA Modules:
  0.0 78.0 jit_solution(14464482616808808658)
XLA Ops:
  0.0 5.3 %place.1 = (bf16[32,49,8,128]{3,2,1,0:T(8,128)(2,1)S(1)}, s32[1,1024]{1,0:T(1,128)S(1)}, s32[1,1024]{1,0:T(1,128)S(1)}) custom-call(bf16[1024,1024]{1,0:T(8,128)(2,1)} %rows_hbm.1, s32[1,1024]{1,0:T(1,128)} %bitcast.13, s32[1,1024]{1,0:T(1,128)} %bitcast.14), custom_call_target="tpu_custom_call" | custom-call | tf_op jit(solution)/shard_map/place/pallas_call | solution.py:329
  5.3 54.2 %all_to_all.10 = bf16[128,49,2,128]{3,2,1,0:T(2,128)(2,1)S(1)} all-to-all(bf16[128,49,2,128]{3,2,1,0:T(2,128)(2,1)S(1)} %bitcast.10), channel_id=1, replica_groups=mesh['grp'=32,'blk'=4] {'grp','blk'}, dimensions={0} | all-to-all | bytes 6422528 | tf_op jit(solution)/shard_map/all_to_all | solution.py:355
  59.5 4.2 %score.1 = f32[128,128]{1,0:T(8,128)S(1)} custom-call(bf16[32,49,8,128]{3,2,1,0:T(8,128)(2,1)S(1)} %bitcast.9), custom_call_target="tpu_custom_call" | custom-call | tf_op jit(solution)/shard_map/score/pallas_call | solution.py:362
  63.7 13.5 %all_to_all.11 = f32[128,1,128]{2,1,0:T(1,128)S(1)} all-to-all(f32[128,1,128]{2,1,0:T(1,128)S(1)} %bitcast.11), channel_id=1, replica_groups=mesh['grp'=32,'blk'=4] {'grp','blk'}, dimensions={0} | all-to-all | bytes 131072 | tf_op jit(solution)/shard_map/all_to_all | solution.py:376
  77.2 0.8 %pick.1 = f32[1,1024]{1,0:T(1,128)} custom-call(f32[128,128]{1,0:T(8,128)S(1)} %bitcast.12, s32[1,1024]{1,0:T(1,128)S(1)} %get-tuple-element.9.label_ref, s32[1,1024]{1,0:T(1,128)S(1)} %get-tuple-element.10.lane_ref), custom_call_target="tpu_custom_call" | custom-call | tf_op jit(solution)/shard_map/pick/pallas_call | solution.py:379

commit v5 on v4

--- a/solution.py
+++ b/solution.py
@@ -159,7 +159,9 @@
             put(MAIN + n * step // 128 + k, folded[:, :, k * 128 : (k + 1) * 128])
 
 
-def score_kernel(got_ref, best_ref, member, digits, column, row_best, col_best, results):
+def score_kernel(
+    got_ref, best_ref, member, digits, column, row_best, col_best, results, ordered
+):
     groups = got_ref.shape[0]
     devices = groups * GROUP
     docs, width = member.shape
@@ -291,11 +293,18 @@
         results[at, :] = jnp.maximum(best, row_best[at, :])
     lane = lax.broadcasted_iota(jnp.int32, (groups, 128), 1)
     for index, turns in enumerate(TURNS):
-        best_ref[pl.ds((me + turns) & 3, groups, stride=GROUP), :] = jnp.where(
+        best = jnp.where(
             lane < MAIN,
             results[pl.ds(index, groups, stride=GROUP), :],
             results[pl.ds(devices + index // 2, groups, stride=2), :],
         )
+        for e in range(GROUP):
+
+            @pl.when(me == e)
+            def _():
+                ordered[pl.ds((e + turns) % GROUP, groups, stride=GROUP), :] = best
+
+    best_ref[...] = ordered[:devices, :]
 
 
 def pick_kernel(got_ref, label_ref, lane_ref, out_ref):
@@ -368,7 +377,8 @@
             pltpu.VMEM((docs, 128), jnp.float32),
             pltpu.VMEM((docs // 8, 128), jnp.float32),
             pltpu.VMEM((8, docs), jnp.float32),
-            pltpu.VMEM((docs // 8, 128), jnp.float32),
+            pltpu.VMEM((docs // 8 + 8, 128), jnp.float32),
+            pltpu.VMEM((devices + 8, 128), jnp.float32),
         ],
         compiler_params=params,
         name="score",

time: 78.2 us -> 78.3 us (level)
  no operation moved by 1% of the time
where the time goes in v5:
time: 78.3 us; the launch traced here: 78.1 us
  blocking collectives  67.7 us (86%)
  Pallas kernels  10.3 us (13%)
    all_to_all x1, blocking collectives, shards(): lax.all_to_all(outgoing.reshape(devices, units, 2, 128), ('grp', 'blk'),...  54.2 us
    all_to_all x1, blocking collectives, shards(): lax.all_to_all(best.reshape(devices, 1, 128), ('grp', 'blk'), split_axis=...  13.5 us
    pallas_call x1, Pallas kernels, shards(): pl.pallas_call(place_kernel, in_specs=[in_hbm] * 3, out_shape=[jax.ShapeD...  5.27 us
    pallas_call x1, Pallas kernels, shards(): pl.pallas_call(score_kernel, out_shape=jax.ShapeDtypeStruct((devices, 128...  4.24 us

profile of v5, /device:TPU:1, one launch (start us, length us, event | category | flops | bytes accessed | tf_op | source)
XLA Modules:
  0.0 78.1 jit_solution(12507454057481531958)
XLA Ops:
  0.0 5.3 %place.1 = (bf16[32,49,8,128]{3,2,1,0:T(8,128)(2,1)S(1)}, s32[1,1024]{1,0:T(1,128)S(1)}, s32[1,1024]{1,0:T(1,128)S(1)}) custom-call(bf16[1024,1024]{1,0:T(8,128)(2,1)} %rows_hbm.1, s32[1,1024]{1,0:T(1,128)} %bitcast.13, s32[1,1024]{1,0:T(1,128)} %bitcast.14), custom_call_target="tpu_custom_call" | custom-call | tf_op jit(solution)/shard_map/place/pallas_call | solution.py:338
  5.3 54.2 %all_to_all.10 = bf16[128,49,2,128]{3,2,1,0:T(2,128)(2,1)S(1)} all-to-all(bf16[128,49,2,128]{3,2,1,0:T(2,128)(2,1)S(1)} %bitcast.10), channel_id=1, replica_groups=mesh['grp'=32,'blk'=4] {'grp','blk'}, dimensions={0} | all-to-all | bytes 6422528 | tf_op jit(solution)/shard_map/all_to_all | solution.py:364
  59.5 4.2 %score.1 = f32[128,128]{1,0:T(8,128)S(1)} custom-call(bf16[32,49,8,128]{3,2,1,0:T(8,128)(2,1)S(1)} %bitcast.9), custom_call_target="tpu_custom_call" | custom-call | tf_op jit(solution)/shard_map/score/pallas_call | solution.py:371
  63.8 13.5 %all_to_all.11 = f32[128,1,128]{2,1,0:T(1,128)S(1)} all-to-all(f32[128,1,128]{2,1,0:T(1,128)S(1)} %bitcast.11), channel_id=1, replica_groups=mesh['grp'=32,'blk'=4] {'grp','blk'}, dimensions={0} | all-to-all | bytes 131072 | tf_op jit(solution)/shard_map/all_to_all | solution.py:386
  77.3 0.8 %pick.1 = f32[1,1024]{1,0:T(1,128)} custom-call(f32[128,128]{1,0:T(8,128)S(1)} %bitcast.12, s32[1,1024]{1,0:T(1,128)S(1)} %get-tuple-element.9.label_ref, s32[1,1024]{1,0:T(1,128)S(1)} %get-tuple-element.10.lane_ref), custom_call_target="tpu_custom_call" | custom-call | tf_op jit(solution)/shard_map/pick/pallas_call | solution.py:389

commit v6 on v5

--- a/solution.py
+++ b/solution.py
@@ -16,13 +16,14 @@
 
 def place_kernel(
     rows_hbm, label_hbm, order_hbm, out_ref, lane_ref, label_ref,
-    rows, order_ref, unit, pick, members, marks, places, sems,
+    rows, order_ref, pick, tail_pick, members, marks, places, sems, *unit,
 ):
     count, width = rows.shape
     groups = out_ref.shape[0]
     devices = groups * GROUP
     half = width // 2
     main_rows, tail_rows = devices * MAIN, devices * TAIL
+    step = unit[0].shape[1]
     parts = 4
     part_rows = count // parts
     copies = [
@@ -76,7 +77,7 @@
     index = index.reshape(8, 16, count)
     one, zero = jnp.ones((), jnp.bfloat16), jnp.zeros((), jnp.bfloat16)
 
-    def choose(first, chosen, code):
+    def choose(pick, first, chosen, code):
         code = jnp.where(chosen, code, -1).astype(jnp.float32)
         code = jnp.broadcast_to(code, (16, count)).astype(jnp.bfloat16)
         pick[first : first + 128, :] = jnp.where(index == code[None], one, zero).reshape(
@@ -85,13 +86,15 @@
 
     for block in range(main_rows // 128):
         choose(
+            pick,
             block * 128,
             ((labels >> 4) == block) & (position < MAIN),
             (labels & 15) * MAIN + position,
         )
     for block in range(tail_rows // 128):
         choose(
-            main_rows + block * 128,
+            tail_pick,
+            block * 128,
             ((labels >> 5) == block) & (position >= MAIN),
             (labels & 31) * TAIL + position - MAIN,
         )
@@ -105,7 +108,9 @@
         scale = lax.rsqrt(
             jnp.mean(values * values, axis=1, keepdims=True) + 1e-06
         ) * width ** (-0.5)
-        unit[at, :] = (values * scale).astype(jnp.bfloat16)
+        values = (values * scale).astype(jnp.bfloat16)
+        for n, columns in enumerate(unit):
+            columns[at, :] = values[:, n * step : (n + 1) * step]
 
     turn = lax.broadcasted_iota(jnp.int32, (8, 128), 0) >> 1
 
@@ -128,22 +133,21 @@
                     mixed = jnp.where(turn >= e, values[group, e], mixed)
                 out_ref[group, CAP * e] = mixed.astype(jnp.bfloat16)
 
-    step = 256
     upper = lax.broadcasted_iota(jnp.int32, (devices // 2, 8, step), 1) >= 4
     for n in range(half // step):
         ends = (n * step, half + n * step)
         for first in ends:
             main = jnp.dot(
-                pick[:main_rows, :],
-                unit[:, first : first + step],
+                pick[...],
+                unit[first // step][...],
                 preferred_element_type=jnp.float32,
             )
             for k in range(step // 128):
                 put(first // 128 + k, main[:, k * 128 : (k + 1) * 128])
         low, high = (
             jnp.dot(
-                pick[main_rows:, :],
-                unit[:, first : first + step],
+                tail_pick[...],
+                unit[first // step][...],
                 preferred_element_type=jnp.float32,
             ).reshape(devices // 2, 8, step)
             for first in ends
@@ -160,11 +164,12 @@
 
 
 def score_kernel(
-    got_ref, best_ref, member, digits, column, row_best, col_best, results, ordered
+    got_ref, best_ref, digits, column, row_best, results, ordered, *member
 ):
     groups = got_ref.shape[0]
     devices = groups * GROUP
-    docs, width = member.shape
+    step, width = member[0].shape
+    docs = step * len(member)
     pieces = width // 128
     main_rows = devices * MAIN
     last = GROUP * CAP
@@ -177,6 +182,10 @@
 
     def both(a, b):
         return jnp.concatenate([a, b], axis=0).astype(jnp.bfloat16)
+
+    def put(first, t, values):
+        at = slice(first % step, first % step + 16)
+        member[first // step][at, t * 128 : (t + 1) * 128] = values
 
     for group in range(groups):
         chunks = []
@@ -207,7 +216,7 @@
             a, b = TURNS[2 * k], TURNS[2 * k + 1]
             at = slice(group * 32 + k * 16, group * 32 + k * 16 + 16)
             for t in range(pieces):
-                member[at, t * 128 : (t + 1) * 128] = both(chunks[a][t], chunks[b][t])
+                put(at.start, t, both(chunks[a][t], chunks[b][t]))
             digits[at, :] = both(
                 *(
                     jnp.where(owner == ((line - 2 * turns) & 7), places[turns], 0.0)
@@ -217,14 +226,13 @@
         at = slice(main_rows + group * 16, main_rows + group * 16 + 16)
         for t in range(pieces // 2):
             a, b, c, d = (chunks[turns][MAIN + t] for turns in range(GROUP))
-            member[at, t * 128 : (t + 1) * 128] = both(
-                jnp.where(first_half, a, c), jnp.where(inner, b, d)
-            )
+            put(at.start, t, both(jnp.where(first_half, a, c), jnp.where(inner, b, d)))
             t = t + pieces // 2
-            member[at, t * 128 : (t + 1) * 128] = both(
+            high = both(
                 pltpu.roll(jnp.where(first_half, c, a), 4, 0),
                 pltpu.roll(jnp.where(inner, d, b), 4, 0),
             )
+            put(at.start, t, high)
         digits[at, :] = both(
             jnp.where(
                 owner == MAIN + (line & 3), jnp.where(first_half, places[0], places[2]), 0.0
@@ -250,15 +258,13 @@
     place_row = lax.dot_general(
         weights((8, 128), 1), digits[...], NT, preferred_element_type=jnp.float32
     )
-    step = 256
-    col_best[...] = jnp.full_like(col_best, -1.0)
+    col_best = [jnp.full((8, 128), -1.0, jnp.float32)] * (docs // 128)
     for i in range(docs // step):
         mine = slice(i * step, (i + 1) * step)
         best = jnp.full((step, 128), -1.0, jnp.float32)
         for j in range(i + 1):
-            theirs = slice(j * step, (j + 1) * step)
             scores = lax.dot_general(
-                member[mine, :], member[theirs, :], NT, preferred_element_type=jnp.float32
+                member[i][...], member[j][...], NT, preferred_element_type=jnp.float32
             )
             for k in range(step // 128):
                 at = j * step + k * 128
@@ -267,8 +273,8 @@
                 best = jnp.maximum(best, jnp.where(earlier, part, -1.0))
                 if j != i:
                     other = jnp.where(earlier, -1.0, part)
-                    col_best[:, at : at + 128] = jnp.maximum(
-                        col_best[:, at : at + 128],
+                    col_best[at // 128] = jnp.maximum(
+                        col_best[at // 128],
                         jnp.max(other.reshape(step // 8, 8, 128), axis=0),
                     )
         best = jnp.broadcast_to(jnp.max(best, axis=1, keepdims=True), (step, 128))
@@ -285,7 +291,7 @@
         == lax.broadcasted_iota(jnp.int32, (16, 128), 0)
     )
     for block in range(docs // 128):
-        best = jnp.max(col_best[:, block * 128 : (block + 1) * 128], axis=0, keepdims=True)
+        best = jnp.max(col_best[block], axis=0, keepdims=True)
         best = jnp.where(own, jnp.broadcast_to(best, (16, 128)), -2.0)
         for shift in (64, 32, 16, 8):
             best = jnp.maximum(best, pltpu.roll(best, shift, 1))
@@ -332,7 +338,7 @@
     rows, width = embeddings.shape
     devices = lax.axis_size("grp") * lax.axis_size("blk")
     groups, units = devices // GROUP, GROUP * CAP + 1
-    docs = devices * CAP
+    docs, step = devices * CAP, 256
     params = pltpu.CompilerParams(vmem_limit_bytes=VMEM_LIMIT)
     in_hbm = pl.BlockSpec(memory_space=pltpu.HBM)
     outgoing, lane_row, label_row = pl.pallas_call(
@@ -346,13 +352,14 @@
         scratch_shapes=[
             pltpu.VMEM((rows, width), jnp.bfloat16),
             pltpu.VMEM((1, rows), jnp.int32),
-            pltpu.VMEM((rows, width), jnp.bfloat16),
-            pltpu.VMEM((docs, rows), jnp.bfloat16),
+            pltpu.VMEM((devices * MAIN, rows), jnp.bfloat16),
+            pltpu.VMEM((devices * TAIL, rows), jnp.bfloat16),
             pltpu.VMEM((devices, rows), jnp.bfloat16),
             pltpu.VMEM((128, rows), jnp.bfloat16),
             pltpu.VMEM((devices, 128), jnp.float32),
             pltpu.SemaphoreType.DMA((6,)),
-        ],
+        ]
+        + [pltpu.VMEM((rows, step), jnp.bfloat16)] * (width // step),
         compiler_params=params,
         name="place",
     )(
@@ -372,14 +379,13 @@
         score_kernel,
         out_shape=jax.ShapeDtypeStruct((devices, 128), jnp.float32),
         scratch_shapes=[
-            pltpu.VMEM((docs, width), jnp.bfloat16),
             pltpu.VMEM((docs, 128), jnp.bfloat16),
             pltpu.VMEM((docs, 128), jnp.float32),
             pltpu.VMEM((docs // 8, 128), jnp.float32),
-            pltpu.VMEM((8, docs), jnp.float32),
             pltpu.VMEM((docs // 8 + 8, 128), jnp.float32),
             pltpu.VMEM((devices + 8, 128), jnp.float32),
-        ],
+        ]
+        + [pltpu.VMEM((step, width), jnp.bfloat16)] * (docs // step),
         compiler_params=params,
         name="score",
     )(got.reshape(groups, units, 8, 128))

time: 78.3 us -> 78 us (level)
  no operation moved by 1% of the time
where the time goes in v6:
time: 78 us; the launch traced here: 77.9 us
  blocking collectives  67.7 us (87%)
  Pallas kernels  10.1 us (13%)
    all_to_all x1, blocking collectives, shards(): lax.all_to_all(outgoing.reshape(devices, units, 2, 128), ('grp', 'blk'),...  54.2 us
    all_to_all x1, blocking collectives, shards(): lax.all_to_all(best.reshape(devices, 1, 128), ('grp', 'blk'), split_axis=...  13.5 us
    pallas_call x1, Pallas kernels, shards(): pl.pallas_call(place_kernel, in_specs=[in_hbm] * 3, out_shape=[jax.ShapeD...  5.27 us
    pallas_call x1, Pallas kernels, shards(): pl.pallas_call(score_kernel, out_shape=jax.ShapeDtypeStruct((devices, 128...  3.99 us

profile of v6, /device:TPU:1, one launch (start us, length us, event | category | flops | bytes accessed | tf_op | source)
XLA Modules:
  0.0 77.9 jit_solution(1917348184457206350)
XLA Ops:
  0.0 5.3 %place.1 = (bf16[32,49,8,128]{3,2,1,0:T(8,128)(2,1)S(1)}, s32[1,1024]{1,0:T(1,128)S(1)}, s32[1,1024]{1,0:T(1,128)S(1)}) custom-call(bf16[1024,1024]{1,0:T(8,128)(2,1)} %rows_hbm.1, s32[1,1024]{1,0:T(1,128)} %bitcast.13, s32[1,1024]{1,0:T(1,128)} %bitcast.14), custom_call_target="tpu_custom_call" | custom-call | tf_op jit(solution)/shard_map/place/pallas_call | solution.py:344
  5.3 54.2 %all_to_all.10 = bf16[128,49,2,128]{3,2,1,0:T(2,128)(2,1)S(1)} all-to-all(bf16[128,49,2,128]{3,2,1,0:T(2,128)(2,1)S(1)} %bitcast.10), channel_id=1, replica_groups=mesh['grp'=32,'blk'=4] {'grp','blk'}, dimensions={0} | all-to-all | bytes 6422528 | tf_op jit(solution)/shard_map/all_to_all | solution.py:371
  59.5 4.0 %score.1 = f32[128,128]{1,0:T(8,128)S(1)} custom-call(bf16[32,49,8,128]{3,2,1,0:T(8,128)(2,1)S(1)} %bitcast.9), custom_call_target="tpu_custom_call" | custom-call | tf_op jit(solution)/shard_map/score/pallas_call | solution.py:378
  63.5 13.5 %all_to_all.11 = f32[128,1,128]{2,1,0:T(1,128)S(1)} all-to-all(f32[128,1,128]{2,1,0:T(1,128)S(1)} %bitcast.11), channel_id=1, replica_groups=mesh['grp'=32,'blk'=4] {'grp','blk'}, dimensions={0} | all-to-all | bytes 131072 | tf_op jit(solution)/shard_map/all_to_all | solution.py:392
  77.0 0.8 %pick.1 = f32[1,1024]{1,0:T(1,128)} custom-call(f32[128,128]{1,0:T(8,128)S(1)} %bitcast.12, s32[1,1024]{1,0:T(1,128)S(1)} %get-tuple-element.9.label_ref, s32[1,1024]{1,0:T(1,128)S(1)} %get-tuple-element.10.lane_ref), custom_call_target="tpu_custom_call" | custom-call | tf_op jit(solution)/shard_map/pick/pallas_call | solution.py:395

commit v7 on v6

--- a/solution.py
+++ b/solution.py
@@ -262,21 +262,35 @@
     for i in range(docs // step):
         mine = slice(i * step, (i + 1) * step)
         best = jnp.full((step, 128), -1.0, jnp.float32)
-        for j in range(i + 1):
+        half = step // 2
+
+        def take(best, rows, scores, at, both_ways):
+            earlier = place_row[0:1, at : at + 128] < column[rows, :]
+            best = jnp.maximum(best, jnp.where(earlier, scores, -1.0))
+            if both_ways:
+                other = jnp.where(earlier, -1.0, scores).reshape(-1, 8, 128)
+                col_best[at // 128] = jnp.maximum(col_best[at // 128], jnp.max(other, axis=0))
+            return best
+
+        for j in range(i):
             scores = lax.dot_general(
                 member[i][...], member[j][...], NT, preferred_element_type=jnp.float32
             )
             for k in range(step // 128):
-                at = j * step + k * 128
                 part = scores[:, k * 128 : (k + 1) * 128]
-                earlier = place_row[0:1, at : at + 128] < column[mine, :]
-                best = jnp.maximum(best, jnp.where(earlier, part, -1.0))
-                if j != i:
-                    other = jnp.where(earlier, -1.0, part)
-                    col_best[at // 128] = jnp.maximum(
-                        col_best[at // 128],
-                        jnp.max(other.reshape(step // 8, 8, 128), axis=0),
-                    )
+                best = take(best, mine, part, j * step + k * 128, True)
+        low = lax.dot_general(
+            member[i][half:, :], member[i][...], NT, preferred_element_type=jnp.float32
+        )
+        high = lax.dot_general(
+            member[i][:half, :], member[i][:half, :], NT, preferred_element_type=jnp.float32
+        )
+        first = i * step
+        top = take(best[:half], slice(first, first + half), high, first, False)
+        rows = slice(first + half, first + step)
+        bottom = take(best[half:], rows, low[:, :half], first, True)
+        bottom = take(bottom, rows, low[:, half:], first + half, False)
+        best = jnp.concatenate([top, bottom], axis=0)
         best = jnp.broadcast_to(jnp.max(best, axis=1, keepdims=True), (step, 128))
         place = lax.broadcasted_iota(jnp.int32, (step, 128), 0) & 7
         if i * step >= main_rows:

time: 78 us -> 78.3 us (level)
  no operation moved by 1% of the time
where the time goes in v7:
time: 78.3 us; the launch traced here: 78.2 us
  blocking collectives  67.7 us (86%)
  Pallas kernels  10.4 us (13%)
    all_to_all x1, blocking collectives, shards(): lax.all_to_all(outgoing.reshape(devices, units, 2, 128), ('grp', 'blk'),...  54.2 us
    all_to_all x1, blocking collectives, shards(): lax.all_to_all(best.reshape(devices, 1, 128), ('grp', 'blk'), split_axis=...  13.5 us
    pallas_call x1, Pallas kernels, shards(): pl.pallas_call(place_kernel, in_specs=[in_hbm] * 3, out_shape=[jax.ShapeD...  5.27 us
    pallas_call x1, Pallas kernels, shards(): pl.pallas_call(score_kernel, out_shape=jax.ShapeDtypeStruct((devices, 128...  4.31 us

profile of v7, /device:TPU:1, one launch (start us, length us, event | category | flops | bytes accessed | tf_op | source)
XLA Modules:
  0.0 78.2 jit_solution(5108517317203793351)
XLA Ops:
  0.0 5.3 %place.1 = (bf16[32,49,8,128]{3,2,1,0:T(8,128)(2,1)S(1)}, s32[1,1024]{1,0:T(1,128)S(1)}, s32[1,1024]{1,0:T(1,128)S(1)}) custom-call(bf16[1024,1024]{1,0:T(8,128)(2,1)} %rows_hbm.1, s32[1,1024]{1,0:T(1,128)} %bitcast.13, s32[1,1024]{1,0:T(1,128)} %bitcast.14), custom_call_target="tpu_custom_call" | custom-call | tf_op jit(solution)/shard_map/place/pallas_call | solution.py:358
  5.3 54.2 %all_to_all.10 = bf16[128,49,2,128]{3,2,1,0:T(2,128)(2,1)S(1)} all-to-all(bf16[128,49,2,128]{3,2,1,0:T(2,128)(2,1)S(1)} %bitcast.10), channel_id=1, replica_groups=mesh['grp'=32,'blk'=4] {'grp','blk'}, dimensions={0} | all-to-all | bytes 6422528 | tf_op jit(solution)/shard_map/all_to_all | solution.py:385
  59.5 4.3 %score.1 = f32[128,128]{1,0:T(8,128)S(1)} custom-call(bf16[32,49,8,128]{3,2,1,0:T(8,128)(2,1)S(1)} %bitcast.9), custom_call_target="tpu_custom_call" | custom-call | tf_op jit(solution)/shard_map/score/pallas_call | solution.py:392
  63.8 13.5 %all_to_all.11 = f32[128,1,128]{2,1,0:T(1,128)S(1)} all-to-all(f32[128,1,128]{2,1,0:T(1,128)S(1)} %bitcast.11), channel_id=1, replica_groups=mesh['grp'=32,'blk'=4] {'grp','blk'}, dimensions={0} | all-to-all | bytes 131072 | tf_op jit(solution)/shard_map/all_to_all | solution.py:406
  77.3 0.8 %pick.1 = f32[1,1024]{1,0:T(1,128)} custom-call(f32[128,128]{1,0:T(8,128)S(1)} %bitcast.12, s32[1,1024]{1,0:T(1,128)S(1)} %get-tuple-element.9.label_ref, s32[1,1024]{1,0:T(1,128)S(1)} %get-tuple-element.10.lane_ref), custom_call_target="tpu_custom_call" | custom-call | tf_op jit(solution)/shard_map/pick/pallas_call | solution.py:409

commit v8 on v6

--- a/solution.py
+++ b/solution.py
@@ -164,10 +164,11 @@
 
 
 def score_kernel(
-    got_ref, best_ref, digits, column, row_best, results, ordered, *member
+    got_ref, best_ref, digits, row_best, results, ordered, *blocks
 ):
     groups = got_ref.shape[0]
     devices = groups * GROUP
+    member, column = blocks[: len(blocks) // 2], blocks[len(blocks) // 2 :]
     step, width = member[0].shape
     docs = step * len(member)
     pieces = width // 128
@@ -252,15 +253,17 @@
         )
         return jnp.where(at < 4 * CAP, weight, 0.0).astype(jnp.bfloat16)
 
-    column[...] = jnp.dot(
-        digits[...], weights((128, 128), 0), preferred_element_type=jnp.float32
-    )
+    for i, places in enumerate(column):
+        places[...] = jnp.dot(
+            digits[i * step : (i + 1) * step, :],
+            weights((128, 128), 0),
+            preferred_element_type=jnp.float32,
+        )
     place_row = lax.dot_general(
         weights((8, 128), 1), digits[...], NT, preferred_element_type=jnp.float32
     )
     col_best = [jnp.full((8, 128), -1.0, jnp.float32)] * (docs // 128)
     for i in range(docs // step):
-        mine = slice(i * step, (i + 1) * step)
         best = jnp.full((step, 128), -1.0, jnp.float32)
         for j in range(i + 1):
             scores = lax.dot_general(
@@ -269,7 +272,7 @@
             for k in range(step // 128):
                 at = j * step + k * 128
                 part = scores[:, k * 128 : (k + 1) * 128]
-                earlier = place_row[0:1, at : at + 128] < column[mine, :]
+                earlier = place_row[0:1, at : at + 128] < column[i][...]
                 best = jnp.maximum(best, jnp.where(earlier, part, -1.0))
                 if j != i:
                     other = jnp.where(earlier, -1.0, part)
@@ -380,12 +383,12 @@
         out_shape=jax.ShapeDtypeStruct((devices, 128), jnp.float32),
         scratch_shapes=[
             pltpu.VMEM((docs, 128), jnp.bfloat16),
-            pltpu.VMEM((docs, 128), jnp.float32),
             pltpu.VMEM((docs // 8, 128), jnp.float32),
             pltpu.VMEM((docs // 8 + 8, 128), jnp.float32),
             pltpu.VMEM((devices + 8, 128), jnp.float32),
         ]
-        + [pltpu.VMEM((step, width), jnp.bfloat16)] * (docs // step),
+        + [pltpu.VMEM((step, width), jnp.bfloat16)] * (docs // step)
+        + [pltpu.VMEM((step, 128), jnp.float32)] * (docs // step),
         compiler_params=params,
         name="score",
     )(got.reshape(groups, units, 8, 128))

time: 78 us -> 78 us (level)
  no operation moved by 1% of the time
where the time goes in v8:
time: 78 us; the launch traced here: 77.9 us
  blocking collectives  67.7 us (87%)
  Pallas kernels  10.1 us (13%)
    all_to_all x1, blocking collectives, shards(): lax.all_to_all(outgoing.reshape(devices, units, 2, 128), ('grp', 'blk'),...  54.2 us
    all_to_all x1, blocking collectives, shards(): lax.all_to_all(best.reshape(devices, 1, 128), ('grp', 'blk'), split_axis=...  13.5 us
    pallas_call x1, Pallas kernels, shards(): pl.pallas_call(place_kernel, in_specs=[in_hbm] * 3, out_shape=[jax.ShapeD...  5.27 us
    pallas_call x1, Pallas kernels, shards(): pl.pallas_call(score_kernel, out_shape=jax.ShapeDtypeStruct((devices, 128...  3.99 us

profile of v8, /device:TPU:1, one launch (start us, length us, event | category | flops | bytes accessed | tf_op | source)
XLA Modules:
  0.0 77.9 jit_solution(1537461839515878613)
XLA Ops:
  0.0 5.3 %place.1 = (bf16[32,49,8,128]{3,2,1,0:T(8,128)(2,1)S(1)}, s32[1,1024]{1,0:T(1,128)S(1)}, s32[1,1024]{1,0:T(1,128)S(1)}) custom-call(bf16[1024,1024]{1,0:T(8,128)(2,1)} %rows_hbm.1, s32[1,1024]{1,0:T(1,128)} %bitcast.13, s32[1,1024]{1,0:T(1,128)} %bitcast.14), custom_call_target="tpu_custom_call" | custom-call | tf_op jit(solution)/shard_map/place/pallas_call | solution.py:347
  5.3 54.2 %all_to_all.10 = bf16[128,49,2,128]{3,2,1,0:T(2,128)(2,1)S(1)} all-to-all(bf16[128,49,2,128]{3,2,1,0:T(2,128)(2,1)S(1)} %bitcast.10), channel_id=1, replica_groups=mesh['grp'=32,'blk'=4] {'grp','blk'}, dimensions={0} | all-to-all | bytes 6422528 | tf_op jit(solution)/shard_map/all_to_all | solution.py:374
  59.5 4.0 %score.1 = f32[128,128]{1,0:T(8,128)S(1)} custom-call(bf16[32,49,8,128]{3,2,1,0:T(8,128)(2,1)S(1)} %bitcast.9), custom_call_target="tpu_custom_call" | custom-call | tf_op jit(solution)/shard_map/score/pallas_call | solution.py:381
  63.5 13.5 %all_to_all.11 = f32[128,1,128]{2,1,0:T(1,128)S(1)} all-to-all(f32[128,1,128]{2,1,0:T(1,128)S(1)} %bitcast.11), channel_id=1, replica_groups=mesh['grp'=32,'blk'=4] {'grp','blk'}, dimensions={0} | all-to-all | bytes 131072 | tf_op jit(solution)/shard_map/all_to_all | solution.py:395
  77.0 0.8 %pick.1 = f32[1,1024]{1,0:T(1,128)} custom-call(f32[128,128]{1,0:T(8,128)S(1)} %bitcast.12, s32[1,1024]{1,0:T(1,128)S(1)} %get-tuple-element.9.label_ref, s32[1,1024]{1,0:T(1,128)S(1)} %get-tuple-element.10.lane_ref), custom_call_target="tpu_custom_call" | custom-call | tf_op jit(solution)/shard_map/pick/pallas_call | solution.py:398
